TPU v7x, 256 devices: a whole 4x4x8 slice. The times are simulated.
256 devices in a mesh: relay: 4 (over x), expert: 16 (over z, core), tensor: 4 (over y).
Axes of the slice: x: 4, y: 4, z: 8, core: 2. Of those that a mesh axis runs over, the one named last changes fastest.
Arguments:
- gate_weight_stack: bfloat16 [16, 4096, 768], P('expert', ('relay', 'tensor')), may hold values from -6 to 6
- up_weight_stack: bfloat16 [16, 4096, 768], P('expert', ('relay', 'tensor')), may hold values from -6 to 6
- down_weight_stack: bfloat16 [16, 4096, 768], P('expert', ('relay', 'tensor')), may hold values from -6 to 6
- adapter_width_factors: bfloat16 [16, 3, 4096, 64], P('expert', None, ('relay', 'tensor')), may hold values from -6 to 6
- adapter_hidden_factors: bfloat16 [16, 3, 64, 768], P('expert', None, None, 'tensor'), may hold values from -0.75 to 0.75
- placement: int32 [16, 16], replicated, may hold values from 0 to 15, as said below
Outputs:
- served: bfloat16 [512, 4, 4, 16, 2304], P('expert', None, 'tensor')
Inputs may be any that keep to these rules, and one draw needn't show every extreme that they name: `placement`: each expert sends at most 2 of its 16 slabs to one owner, and some expert sends exactly 2. Each owner receives at most 32 slabs over all experts, and some owner exactly 32.
All inputs are finite; a program needn't handle non-finite values.
Results may differ from a plain program's by a relative error of at most 0.001.
Values may be sent and summed in bfloat16 or wider, within the bound.
No kernel may reach another device: no remote copies, remote signals or barrier semaphores. Data moves between devices by JAX's collectives and lax.ppermute only.
A program may use at most 64 MiB of HBM per device.

v0:
```python
import functools

import jax
import jax.numpy as jnp
from jax import lax
from jax.experimental import pallas as pl
from jax.experimental.pallas import tpu as pltpu
from jax.sharding import PartitionSpec as P

ADAPTER_SCALE = 0.5
PAIR = 2


def selector(rows, cols, place):
    row = lax.broadcasted_iota(jnp.int32, (rows, cols), 0)
    col = lax.broadcasted_iota(jnp.int32, (rows, cols), 1)
    return jnp.where(col == place(row), 1.0, 0.0).astype(jnp.bfloat16)


def dot(a, b):
    return jnp.dot(a, b, preferred_element_type=jnp.float32)


def dot_t(a, b):
    return lax.dot_general(a, b, (((0,), (0,)), ((), ())), preferred_element_type=jnp.float32)


def merge_kernel(
    index_ref, tensor_ref, gate_hbm, up_hbm, down_hbm, width_hbm, v0, v1, v2, v3,
    self_ref, keep_ref, swap_ref, mixed_ref, plain_ref, merged_ref,
    gate_ref, up_ref, down_ref, width_ref, parts_ref, sems,
):
    parts = [parts_ref.at[j] for j in range(4)]
    loads = [
        pltpu.make_async_copy(src, dst, sems.at[j])
        for j, (src, dst) in enumerate(
            zip(
                (v0, v1, v2, v3, gate_hbm, up_hbm, width_hbm, down_hbm),
                (*parts, gate_ref, up_ref, width_ref, down_ref),
            )
        )
    ]
    for load in loads:
        load.start()
    slabs = index_ref.shape[0]
    rows, hidden = gate_ref.shape
    slab_rows = rows // slabs
    rank = width_ref.shape[1]
    part = parts_ref.shape[3]
    me = tensor_ref[0]
    even = selector(part, 2 * part, lambda row: 2 * row)
    odd = selector(part, 2 * part, lambda row: 2 * row + 1)
    plain_ref[...] = jnp.zeros_like(plain_ref)
    for j, v in enumerate(parts):
        loads[j].wait()
        home = lax.rem(me - j + 4, 4)
        cols = pl.ds(pl.multiple_of(home * (2 * part), 128), 2 * part)
        mixed_ref[:rank, cols] = dot(v[0], even).astype(jnp.bfloat16)
        mixed_ref[rank:, cols] = dot(v[1], odd).astype(jnp.bfloat16)
        shift = lax.rem(home, 2) * part
        pair_cols = pl.ds(pl.multiple_of(lax.div(home, 2) * (2 * part), 128), 2 * part)
        plain_ref[:, pair_cols] += dot(v[2], selector(part, 2 * part, lambda row: row + shift))
    half = 128
    spread = selector(
        2 * half, 2 * half, lambda row: jnp.where(row < half, 2 * row, 2 * (row - half) + 1)
    )
    for load in loads[4:]:
        load.wait()
    both = width_ref[0:2].reshape(2 * rank, rows)
    for block in range(hidden // half):
        src = slice(block * half, (block + 1) * half)
        dst = slice(2 * block * half, 2 * (block + 1) * half)
        weight = dot(jnp.concatenate([gate_ref[:, src], up_ref[:, src]], axis=1), spread)
        delta = dot_t(both, mixed_ref[:, dst])
        merged_ref[:, dst] = (weight + ADAPTER_SCALE * delta).astype(jnp.bfloat16)
    delta = dot_t(width_ref[2], plain_ref[...].astype(jnp.bfloat16))
    merged_ref[:, 2 * hidden :] = (
        down_ref[...].astype(jnp.float32) + ADAPTER_SCALE * delta
    ).astype(jnp.bfloat16)
    bucket = swap_ref.shape[0]
    for k in range(slabs):
        index = index_ref[k]
        block = slice(k * slab_rows, (k + 1) * slab_rows)

        @pl.when(index < PAIR)
        def _():
            self_ref[index] = merged_ref[block, :]

        @pl.when((index >= PAIR) & (index < bucket))
        def _():
            keep_ref[index - PAIR] = merged_ref[block, :]

        @pl.when(index >= bucket)
        def _():
            swap_ref[index - bucket] = merged_ref[block, :]


def merge(index, tensor, gate, up, down, width, parts):
    rows, hidden = gate.shape
    rank = width.shape[1]
    slab_rows = rows // index.shape[0]
    wide = 3 * hidden
    smem = pl.BlockSpec(memory_space=pltpu.SMEM)
    vmem = pl.BlockSpec(memory_space=pltpu.VMEM)

    def slots(n):
        return jax.ShapeDtypeStruct((n, slab_rows, wide), jnp.bfloat16)

    return pl.pallas_call(
        merge_kernel,
        out_shape=[slots(PAIR), slots(16 - PAIR), slots(16)],
        in_specs=[smem, smem] + [pl.BlockSpec(memory_space=pl.ANY)] * 8,
        out_specs=[vmem] * 3,
        scratch_shapes=[
            pltpu.VMEM((2 * rank, 2 * hidden), jnp.bfloat16),
            pltpu.VMEM((rank, hidden), jnp.float32),
            pltpu.VMEM((rows, wide), jnp.bfloat16),
            pltpu.VMEM((rows, hidden), jnp.bfloat16),
            pltpu.VMEM((rows, hidden), jnp.bfloat16),
            pltpu.VMEM((rows, hidden), jnp.bfloat16),
            pltpu.VMEM(width.shape, jnp.bfloat16),
            pltpu.VMEM((4, *parts[0].shape), jnp.bfloat16),
            pltpu.SemaphoreType.DMA((8,)),
        ],
        cost_estimate=pl.CostEstimate(
            flops=2 * rows * wide * 384, bytes_accessed=4_000_000, transcendentals=0
        ),
    )(index, tensor, gate, up, down, width, *parts)


def place_kernel(pieces, first, dest_ref, count_ref, relay_ref, *refs):
    if first:
        bufs, (out_ref, sems, zero_ref, zero_sems) = refs[:-4], refs[-4:]
    else:
        bufs, (_, out_ref, sems) = refs[:-3], refs[-3:]
    groups = out_ref.shape[1]

    def copy(number):
        which, row, entry, shift = pieces[number]
        group = lax.rem(relay_ref[0] + shift, groups)
        dest = jnp.maximum(dest_ref[entry], 0)
        return pltpu.make_async_copy(
            bufs[which].at[row], out_ref.at[dest, group, 0], sems.at[number]
        )

    def blank(slot):
        return pltpu.make_async_copy(zero_ref, out_ref.at[slot], zero_sems.at[slot])

    for number, piece in enumerate(pieces):

        @pl.when(dest_ref[piece[2]] >= 0)
        def _():
            copy(number).start()

    if first:
        zero_ref[...] = jnp.zeros_like(zero_ref)

        @pl.loop(count_ref[0], out_ref.shape[0])
        def _(slot):
            blank(slot).start()

        @pl.loop(count_ref[0], out_ref.shape[0])
        def _(slot):
            blank(slot).wait()

    for number, piece in enumerate(pieces):

        @pl.when(dest_ref[piece[2]] >= 0)
        def _():
            copy(number).wait()


def place(out, pieces, dest, count, relay, bufs, out_shape):
    smem = pl.BlockSpec(memory_space=pltpu.SMEM)
    vmem = pl.BlockSpec(memory_space=pltpu.VMEM)
    anywhere = pl.BlockSpec(memory_space=pl.ANY)
    first = out is None
    scratch = [pltpu.SemaphoreType.DMA((len(pieces),))]
    if first:
        scratch += [
            pltpu.VMEM(out_shape[1:], jnp.bfloat16),
            pltpu.SemaphoreType.DMA((out_shape[0],)),
        ]
    return pl.pallas_call(
        functools.partial(place_kernel, pieces, first),
        out_shape=jax.ShapeDtypeStruct(out_shape, jnp.bfloat16),
        in_specs=[smem] * 3 + [vmem] * len(bufs) + ([] if first else [anywhere]),
        out_specs=anywhere,
        scratch_shapes=scratch,
        input_output_aliases={} if first else {3 + len(bufs): 0},
        cost_estimate=pl.CostEstimate(
            flops=0, bytes_accessed=len(pieces) * 73728, transcendentals=0
        ),
    )(dest, count, relay, *bufs, *([] if first else [out]))


def shift(value, axis, by):
    size = lax.axis_size(axis)
    return lax.ppermute(value, axis, [(i, (i + by) % size) for i in range(size)])


def body(gate, up, down, width, hidden, placement):
    owners = lax.axis_size("expert")
    chips = owners // 2
    slabs = placement.shape[1]
    me = lax.axis_index("expert").astype(jnp.int32)
    targets = lax.dynamic_index_in_dim(placement, me, 0, keepdims=False)
    iota = jnp.arange(slabs, dtype=jnp.int32)
    order = jnp.sum(
        ((targets[None, :] == targets[:, None]) & (iota[None, :] < iota[:, None])).astype(jnp.int32),
        axis=1,
    )
    offset = (targets // 2 - me // 2) % chips
    index = ((targets ^ me) & 1) * (PAIR * chips) + offset * PAIR + order
    hits = jnp.sum((placement == me).astype(jnp.int32), axis=1)
    before = jnp.sum(jnp.where(iota[None, :] < iota[:, None], hits[None, :], 0), axis=1)
    total = jnp.sum(hits)
    pair = jnp.arange(PAIR, dtype=jnp.int32)
    table = jnp.where(pair[None, :] < hits[:, None], before[:, None] + pair[None, :], -1)

    parts = [hidden[0]] + [shift(hidden[0], "tensor", k) for k in (1, 2, 3)]
    own, keep, swap = merge(
        index,
        lax.axis_index("tensor").astype(jnp.int32)[None],
        gate[0], up[0], down[0],
        jnp.swapaxes(width[0], 1, 2),
        parts,
    )
    mate = [(i, i ^ 1) for i in range(owners)]
    got = lax.ppermute(swap, "expert", mate)

    def send(d):
        rows = slice(PAIR * (d - 1), PAIR * d)
        message = jnp.concatenate([keep[rows], got[PAIR * d : PAIR * (d + 1)]], axis=0)
        return shift(message, "expert", 2 * d)

    def pair_of(d):
        return [send(d), send(chips - d)]

    near = jnp.concatenate([own, got[:PAIR]], axis=0)
    steps = [
        ([0], [near], False, False),
        ([1, chips - 1], None, False, False),
        ([2, chips - 2], None, False, False),
        ([3, chips - 3], None, True, False),
        ([4], None, True, True),
        ([], [], False, True),
    ]
    sources = jnp.stack(
        [((me - 2 * d) % owners) ^ core for names, *_ in steps for d in names for core in (0, 1)]
    )
    dest = jnp.sum(
        jnp.where(sources[:, None, None] == iota[None, :, None], table[None], 0), axis=1
    ).reshape(-1)
    relay = lax.axis_index("relay").astype(jnp.int32)[None]
    slab_rows, wide = own.shape[1:]
    out_shape = (owners * PAIR, lax.axis_size("relay"), 1, slab_rows, wide)
    def ring(parts, by):
        arrived = []
        for part in parts:
            message = part[0] if len(part) == 1 else jnp.concatenate(part, axis=0)
            bufs.append(shift(message, "relay", by))
            arrived += [(len(bufs) - 1, row) for row in range(message.shape[0])]
        return arrived

    def messages(front, back, forward, split):
        rest = back + forward
        if split:
            return [front] + ([rest] if rest else [])
        return [front + rest]

    out, bufs, pieces = None, [], []
    forward_right, forward_left, entry, earlier = [], [], 0, []
    for names, items, split, flush in steps:
        items = [send(d) for d in names] if items is None else items
        first, last = items[:1], items[1:]
        from_left = ring(messages(first, last, forward_right, split), 1)
        from_right = ring(
            messages(last, first, forward_left, split)
            if len(items) == 2
            else messages(first, last, forward_left, split),
            -1,
        )
        held = []
        for item in items:
            bufs.append(item)
            held.append([(len(bufs) - 1, row) for row in range(item.shape[0])])
        count = sum(len(rows) for rows in held)
        order = held[0] + (held[1] if len(held) == 2 else []) if held else []
        turned = held[1] + held[0] if len(held) == 2 else order
        half = len(earlier) // 2
        pieces += [(*from_left[count + j], earlier[j], 2) for j in range(half)]
        pieces += [(*from_right[count + j], earlier[half + j], 2) for j in range(half)]
        base = entry
        where = {slot: base + j for j, slot in enumerate(order)}
        for j in range(count):
            pieces += [
                (*order[j], base + j, 0),
                (*from_left[j], where[order[j]], 3),
                (*from_right[j], where[turned[j]], 1),
            ]
        earlier = [base + j for j in range(count)]
        entry += count
        half = count // 2
        forward_right = forward_left = []
        if count:
            left_buf, right_buf = bufs[from_left[0][0]], bufs[from_right[0][0]]
            forward_right = [left_buf if left_buf.shape[0] == half else left_buf[:half]]
            if len(items) == 2:
                forward_left = [right_buf if right_buf.shape[0] == half else right_buf[:half]]
            else:
                forward_left = [right_buf[half:count]]
        if flush:
            out = place(out, pieces, dest, total[None], relay, bufs, out_shape)
            bufs, pieces = [], []
    return out


def solution(mesh):
    return jax.shard_map(
        body,
        mesh=mesh,
        in_specs=(
            P("expert", ("relay", "tensor"), None),
            P("expert", ("relay", "tensor"), None),
            P("expert", ("relay", "tensor"), None),
            P("expert", None, ("relay", "tensor"), None),
            P("expert", None, None, "tensor"),
            P(),
        ),
        out_specs=P("expert", None, "tensor", None, None),
        check_vma=False,
    )
```

profile of v0, /device:TPU:6, one launch (start us, length us, event | category | flops | bytes accessed | tf_op | source)
XLA Modules:
  0.0 142.0 jit_solution(1827574147379475920)
XLA Ops:
  0.0 3.0 %collective-permute-start.2 = (bf16[3,64,192]{2,1,0:T(8,128)(2,1)}, bf16[3,64,192]{2,1,0:T(8,128)(2,1)S(1)}, u32[]{:S(2)}, u32[]{:S(2)}) collective-permute-start(bf16[3,64,192]{2,1,0:T(8,128)(2,1)} %bitcast.34), channel_id=1, source_target_pairs={{0,3},{1,0},{2,1},{3,2},{4,7},{5,4},{6,5},{7,6},{8,11},{9,8},{10,9... | collective-permute-start | bytes 221192 | tf_op jit(solution)/shard_map/ppermute | solution.py:199
  3.0 0.6 collective-permute-start.1
  3.6 1.0 collective-permute-start
  4.6 0.7 dynamic-slice_bitcast_fusion
  5.3 0.2 convert_reduce_fusion.2
  5.5 1.2 fusion.3.index_ref
  6.7 0.8 collective-permute-done.2.v3
  7.5 2.6 %collective-permute-done.1.v2 = bf16[3,64,192]{2,1,0:T(8,128)(2,1)S(1)} collective-permute-done((bf16[3,64,192]{2,1,0:T(8,128)(2,1)}, bf16[3,64,192]{2,1,0:T(8,128)(2,1)S(1)}, u32[]{:S(2)}, u32[]{:S(2)}) %collective-permute-start.1) | collective-permute-done | bytes 73760 | tf_op jit(solution)/shard_map/ppermute | solution.py:199
  10.1 1.0 collective-permute-done.v1
  11.1 0.6 copy-done.23
  11.7 4.9 %shard_map.64 = (bf16[2,16,2304]{2,1,0:T(8,128)(2,1)}, bf16[14,16,2304]{2,1,0:T(8,128)(2,1)}, bf16[16,16,2304]{2,1,0:T(8,128)(2,1)}) custom-call(s32[16]{0:T(128)} %fusion.3.index_ref, s32[1]{0:T(128)} %bitcast.19.tensor_ref, bf16[256,768]{1,0:T(8,128)(2,1)} %bitcast.30, bf16[256,768]{1,0:T(8,128)(2,1)} %bitcast.31, bf16[256,768]{1,0:T(8,128)(2,1)} %bitcast.32, ...), custom_call_target="tpu_custom_call" | custom-call | flops 452984832 | bytes 4000000 | tf_op jit(solution)/shard_map/pallas_call | solution.py:109
  16.7 0.1 collective-permute-start.3
  16.8 1.4 fusion.6
  18.2 1.7 %collective-permute-done.3 = bf16[16,16,2304]{2,1,0:T(8,128)(2,1)S(1)} collective-permute-done((bf16[16,16,2304]{2,1,0:T(8,128)(2,1)}, bf16[16,16,2304]{2,1,0:T(8,128)(2,1)S(1)}, u32[]{:S(2)}, u32[]{:S(2)}) %collective-permute-start.3) | collective-permute-done | bytes 1179680 | tf_op jit(solution)/shard_map/ppermute | solution.py:230
  19.8 0.1 fusion.5
  20.0 0.9 collective-permute-start.10
  20.9 2.4 %collective-permute-start.9 = (bf16[4,16,2304]{2,1,0:T(8,128)(2,1)S(1)}, bf16[4,16,2304]{2,1,0:T(8,128)(2,1)S(1)}, u32[]{:S(2)}, u32[]{:S(2)}) collective-permute-start(bf16[4,16,2304]{2,1,0:T(8,128)(2,1)S(1)} %pad_maximum_fusion.7.refs_2_), channel_id=1, source_target_pairs={{0,64},{64,128},{128,192},{192,0},{1,65},{65,129},{129,193},{193,1... | collective-permute-start | bytes 884744 | tf_op jit(solution)/shard_map/ppermute | solution.py:199
  23.3 2.0 %collective-permute-start.11 = (bf16[4,16,2304]{2,1,0:T(8,128)(2,1)S(1)}, bf16[4,16,2304]{2,1,0:T(8,128)(2,1)S(1)}, u32[]{:S(2)}, u32[]{:S(2)}) collective-permute-start(bf16[4,16,2304]{2,1,0:T(8,128)(2,1)S(1)} %pad_maximum_fusion.8), channel_id=1, source_target_pairs={{0,8},{4,12},{8,16},{12,20},{16,24},{20,28},{24,32},{28,36},{32,40... | collective-permute-start | bytes 884744 | tf_op jit(solution)/shard_map/ppermute | solution.py:199
  25.3 4.0 %collective-permute-start.12 = (bf16[4,16,2304]{2,1,0:T(8,128)(2,1)S(1)}, bf16[4,16,2304]{2,1,0:T(8,128)(2,1)S(1)}, u32[]{:S(2)}, u32[]{:S(2)}) collective-permute-start(bf16[4,16,2304]{2,1,0:T(8,128)(2,1)S(1)} %pad_maximum_fusion.9), channel_id=1, source_target_pairs={{0,56},{4,60},{8,0},{12,4},{16,8},{20,12},{24,16},{28,20},{32,24},... | collective-permute-start | bytes 884744 | tf_op jit(solution)/shard_map/ppermute | solution.py:199
  29.4 0.9 collective-permute-done.10.refs_1_
  30.4 5.6 %collective-permute-done.11.refs_5_ = bf16[4,16,2304]{2,1,0:T(8,128)(2,1)S(1)} collective-permute-done((bf16[4,16,2304]{2,1,0:T(8,128)(2,1)S(1)}, bf16[4,16,2304]{2,1,0:T(8,128)(2,1)S(1)}, u32[]{:S(2)}, u32[]{:S(2)}) %collective-permute-start.11) | collective-permute-done | bytes 294944 | tf_op jit(solution)/shard_map/ppermute | solution.py:199
  36.0 0.2 pad_maximum_fusion.3
  36.2 0.5 copy-done.4
  36.7 0.1 copy-done.5
  36.9 3.2 %collective-permute-start.13 = (bf16[10,16,2304]{2,1,0:T(8,128)(2,1)S(1)}, bf16[10,16,2304]{2,1,0:T(8,128)(2,1)S(1)}, u32[]{:S(2)}, u32[]{:S(2)}) collective-permute-start(bf16[10,16,2304]{2,1,0:T(8,128)(2,1)S(1)} %get-tuple-element.31), channel_id=1, source_target_pairs={{0,64},{64,128},{128,192},{192,0},{1,65},{65,129},{129,193},{193,1... | collective-permute-start | bytes 2211848 | tf_op jit(solution)/shard_map/ppermute | solution.py:199
  40.1 2.3 %collective-permute-start.15 = (bf16[4,16,2304]{2,1,0:T(8,128)(2,1)S(1)}, bf16[4,16,2304]{2,1,0:T(8,128)(2,1)S(1)}, u32[]{:S(2)}, u32[]{:S(2)}) collective-permute-start(bf16[4,16,2304]{2,1,0:T(8,128)(2,1)S(1)} %pad_maximum_fusion.10), channel_id=1, source_target_pairs={{0,16},{4,20},{8,24},{12,28},{16,32},{20,36},{24,40},{28,44},{32,4... | collective-permute-start | bytes 884744 | tf_op jit(solution)/shard_map/ppermute | solution.py:199
  42.4 2.0 %collective-permute-start.16 = (bf16[4,16,2304]{2,1,0:T(8,128)(2,1)S(1)}, bf16[4,16,2304]{2,1,0:T(8,128)(2,1)S(1)}, u32[]{:S(2)}, u32[]{:S(2)}) collective-permute-start(bf16[4,16,2304]{2,1,0:T(8,128)(2,1)S(1)} %pad_maximum_fusion.11), channel_id=1, source_target_pairs={{0,48},{4,52},{8,56},{12,60},{16,0},{20,4},{24,8},{28,12},{32,16},... | collective-permute-start | bytes 884744 | tf_op jit(solution)/shard_map/ppermute | solution.py:199
  44.5 4.4 %collective-permute-start.4 = (bf16[4,16,2304]{2,1,0:T(8,128)(2,1)S(1)}, bf16[4,16,2304]{2,1,0:T(8,128)(2,1)}, u32[]{:S(2)}, u32[]{:S(2)}) collective-permute-start(bf16[4,16,2304]{2,1,0:T(8,128)(2,1)S(1)} %pad_maximum_fusion.6), channel_id=1, source_target_pairs={{0,32},{4,36},{8,40},{12,44},{16,48},{20,52},{24,56},{28,60},{32,0... | collective-permute-start | bytes 884744 | tf_op jit(solution)/shard_map/ppermute | solution.py:199
  48.8 6.6 %collective-permute-done.14.refs_4_ = bf16[10,16,2304]{2,1,0:T(8,128)(2,1)S(1)} collective-permute-done((bf16[10,16,2304]{2,1,0:T(8,128)(2,1)S(1)}, bf16[10,16,2304]{2,1,0:T(8,128)(2,1)S(1)}, u32[]{:S(2)}, u32[]{:S(2)}) %collective-permute-start.14) | collective-permute-done | bytes 737312 | tf_op jit(solution)/shard_map/ppermute | solution.py:199
  55.5 6.5 %collective-permute-done.15.refs_9_ = bf16[4,16,2304]{2,1,0:T(8,128)(2,1)S(1)} collective-permute-done((bf16[4,16,2304]{2,1,0:T(8,128)(2,1)S(1)}, bf16[4,16,2304]{2,1,0:T(8,128)(2,1)S(1)}, u32[]{:S(2)}, u32[]{:S(2)}) %collective-permute-start.15) | collective-permute-done | bytes 294944 | tf_op jit(solution)/shard_map/ppermute | solution.py:199
  62.0 0.2 pad_maximum_fusion.1
  62.2 0.5 copy-done.6
  62.7 0.1 copy-done.7
  62.9 11.7 %collective-permute-start.19 = (bf16[4,16,2304]{2,1,0:T(8,128)(2,1)S(1)}, bf16[4,16,2304]{2,1,0:T(8,128)(2,1)S(1)}, u32[]{:S(2)}, u32[]{:S(2)}) collective-permute-start(bf16[4,16,2304]{2,1,0:T(8,128)(2,1)S(1)} %pad_maximum_fusion.12), channel_id=1, source_target_pairs={{0,24},{4,28},{8,32},{12,36},{16,40},{20,44},{24,48},{28,52},{32,5... | collective-permute-start | bytes 884744 | tf_op jit(solution)/shard_map/ppermute | solution.py:199
  74.6 3.2 %collective-permute-start.17 = (bf16[12,16,2304]{2,1,0:T(8,128)(2,1)S(1)}, bf16[12,16,2304]{2,1,0:T(8,128)(2,1)S(1)}, u32[]{:S(2)}, u32[]{:S(2)}) collective-permute-start(bf16[12,16,2304]{2,1,0:T(8,128)(2,1)S(1)} %get-tuple-element.29), channel_id=1, source_target_pairs={{0,64},{64,128},{128,192},{192,0},{1,65},{65,129},{129,193},{193,1... | collective-permute-start | bytes 2654216 | tf_op jit(solution)/shard_map/ppermute | solution.py:199
  77.9 0.1 collective-permute-start.21
  77.9 10.2 %collective-permute-done.19.refs_15_ = bf16[4,16,2304]{2,1,0:T(8,128)(2,1)S(1)} collective-permute-done((bf16[4,16,2304]{2,1,0:T(8,128)(2,1)S(1)}, bf16[4,16,2304]{2,1,0:T(8,128)(2,1)S(1)}, u32[]{:S(2)}, u32[]{:S(2)}) %collective-permute-start.19) | collective-permute-done | bytes 294944 | tf_op jit(solution)/shard_map/ppermute | solution.py:199
  88.2 0.8 collective-permute-start.20
  89.0 0.7 convert_reduce_fusion
  89.7 1.2 collective-permute-start.7
  90.9 2.0 %collective-permute-start.5 = (bf16[4,16,2304]{2,1,0:T(8,128)(2,1)}, bf16[4,16,2304]{2,1,0:T(8,128)(2,1)S(1)}, u32[]{:S(2)}, u32[]{:S(2)}) collective-permute-start(bf16[4,16,2304]{2,1,0:T(8,128)(2,1)} %collective-permute-done.4.refs_21_), channel_id=1, source_target_pairs={{0,64},{64,128},{128,192},{192,0},{1,65},{65,129},{129,193},{193,1... | collective-permute-start | bytes 884744 | tf_op jit(solution)/shard_map/ppermute | solution.py:199
  93.0 5.2 %collective-permute-done.20.refs_11_ = bf16[4,16,2304]{2,1,0:T(8,128)(2,1)} collective-permute-done((bf16[4,16,2304]{2,1,0:T(8,128)(2,1)S(1)}, bf16[4,16,2304]{2,1,0:T(8,128)(2,1)}, u32[]{:S(2)}, u32[]{:S(2)}) %collective-permute-start.20) | collective-permute-done | bytes 294944 | tf_op jit(solution)/shard_map/ppermute | solution.py:199
  98.2 3.2 %collective-permute-start.25 = (bf16[4,16,2304]{2,1,0:T(8,128)(2,1)}, bf16[4,16,2304]{2,1,0:T(8,128)(2,1)}, u32[]{:S(2)}, u32[]{:S(2)}) collective-permute-start(bf16[4,16,2304]{2,1,0:T(8,128)(2,1)} %collective-permute-done.20.refs_11_), channel_id=1, source_target_pairs={{0,64},{64,128},{128,192},{192,0},{1,65},{65,129},{129,193},{193,1... | collective-permute-start | bytes 884744 | tf_op jit(solution)/shard_map/ppermute | solution.py:199
  101.4 0.9 pad_maximum_fusion.5
  102.4 1.0 pad_maximum_fusion.4
  103.4 3.1 %collective-permute-start.22 = (bf16[8,16,2304]{2,1,0:T(8,128)(2,1)}, bf16[8,16,2304]{2,1,0:T(8,128)(2,1)S(1)}, u32[]{:S(2)}, u32[]{:S(2)}) collective-permute-start(bf16[8,16,2304]{2,1,0:T(8,128)(2,1)} %pad_maximum_fusion.4), channel_id=1, source_target_pairs={{0,64},{64,128},{128,192},{192,0},{1,65},{65,129},{129,193},{193,1... | collective-permute-start | bytes 1769480 | tf_op jit(solution)/shard_map/ppermute | solution.py:199
  106.5 0.1 select_reduce_fusion.1
  106.7 0.1 stack.67
  106.8 0.1 iota_compare_fusion.1
  106.9 0.1 collective-permute-start.8
  107.0 2.1 %collective-permute-done.23.refs_13_ = bf16[4,16,2304]{2,1,0:T(8,128)(2,1)} collective-permute-done((bf16[4,16,2304]{2,1,0:T(8,128)(2,1)S(1)}, bf16[4,16,2304]{2,1,0:T(8,128)(2,1)}, u32[]{:S(2)}, u32[]{:S(2)}) %collective-permute-start.23) | collective-permute-done | bytes 294944 | tf_op jit(solution)/shard_map/ppermute | solution.py:199
  109.1 1.2 collective-permute-start.6
  110.3 0.5 collective-permute-done.25.refs_18_
  110.8 0.3 collective-permute-start.26
  111.1 0.1 select_reduce_fusion
  111.2 0.1 copy.8
  111.3 0.6 reshape.68.dest_ref
  111.9 16.6 %collective-permute-done.26.refs_20_ = bf16[4,16,2304]{2,1,0:T(8,128)(2,1)S(1)} collective-permute-done((bf16[4,16,2304]{2,1,0:T(8,128)(2,1)}, bf16[4,16,2304]{2,1,0:T(8,128)(2,1)S(1)}, u32[]{:S(2)}, u32[]{:S(2)}) %collective-permute-start.26) | collective-permute-done | bytes 294944 | tf_op jit(solution)/shard_map/ppermute | solution.py:199
  128.6 0.7 copy-done.17
  129.3 0.2 copy-done.15
  129.5 0.2 copy-done.16
  129.7 9.7 %shard_map.65.refs_2_ = bf16[32,4,1,16,2304]{4,3,2,1,0:T(8,128)(2,1)} custom-call(s32[32]{0:T(128)} %reshape.68.dest_ref, s32[1]{0:T(128)} %bitcast.16.count_ref, s32[1]{0:T(128)} %bitcast.17.relay_ref, bf16[4,16,2304]{2,1,0:T(8,128)(2,1)} %copy-done.12, bf16[4,16,2304]{2,1,0:T(8,128)(2,1)} %copy-done.11, bf16[4,16,2304]{2,1,0:T(8,128)(2,1)} %copy-done.8, ...), custom_call_target="tpu_custom_call" | custom-call | bytes 9142272 | tf_op jit(solution)/shard_map/pallas_call | solution.py:184
  139.5 0.6 copy-done.19
  140.1 1.7 %shard_map.66 = bf16[32,4,1,16,2304]{4,3,2,1,0:T(8,128)(2,1)} custom-call(s32[32]{0:T(128)} %reshape.68.dest_ref, s32[1]{0:T(128)} %bitcast.16.count_ref, s32[1]{0:T(128)} %bitcast.17.relay_ref, bf16[2,16,2304]{2,1,0:T(8,128)(2,1)} %copy-done.19, bf16[2,16,2304]{2,1,0:T(8,128)(2,1)} %collective-permute-done.8.refs_1_, ...), custom_call_target="tpu_custom_call", output_to_operand_aliasing={{}: (5, {})} | custom-call | bytes 294912 | tf_op jit(solution)/shard_map/pallas_call | solution.py:184
  (74 shorter events, 0.5 us)
Async XLA Ops:
  0.0 7.5 %collective-permute-start.2 = (bf16[3,64,192]{2,1,0:T(8,128)(2,1)}, bf16[3,64,192]{2,1,0:T(8,128)(2,1)S(1)}, u32[]{:S(2)}, u32[]{:S(2)}) collective-permute-start(bf16[3,64,192]{2,1,0:T(8,128)(2,1)} %bitcast.34), channel_id=1, source_target_pairs={{0,3},{1,0},{2,1},{3,2},{4,7},{5,4},{6,5},{7,6},{8,11},{9,8},{10,9... | collective-permute-start | bytes 221192 | tf_op jit(solution)/shard_map/ppermute | solution.py:199
  3.0 7.1 %collective-permute-start.1 = (bf16[3,64,192]{2,1,0:T(8,128)(2,1)}, bf16[3,64,192]{2,1,0:T(8,128)(2,1)S(1)}, u32[]{:S(2)}, u32[]{:S(2)}) collective-permute-start(bf16[3,64,192]{2,1,0:T(8,128)(2,1)} %bitcast.35), channel_id=1, source_target_pairs={{0,2},{1,3},{2,0},{3,1},{4,6},{5,7},{6,4},{7,5},{8,10},{9,11},{10,... | collective-permute-start | bytes 221192 | tf_op jit(solution)/shard_map/ppermute | solution.py:199
  3.6 7.4 %collective-permute-start = (bf16[3,64,192]{2,1,0:T(8,128)(2,1)}, bf16[3,64,192]{2,1,0:T(8,128)(2,1)S(1)}, u32[]{:S(2)}, u32[]{:S(2)}) collective-permute-start(bf16[3,64,192]{2,1,0:T(8,128)(2,1)} %bitcast.36), channel_id=1, source_target_pairs={{0,1},{1,2},{2,3},{3,0},{4,5},{5,6},{6,7},{7,4},{8,9},{9,10},{10,1... | collective-permute-start | bytes 221192 | tf_op jit(solution)/shard_map/ppermute | solution.py:199
  7.5 3.6 %copy-start.21 = (bf16[3,64,192]{2,1,0:T(8,128)(2,1)}, bf16[3,64,192]{2,1,0:T(8,128)(2,1)S(1)}, u32[]{:S(2)}) copy-start(bf16[3,64,192]{2,1,0:T(8,128)(2,1)S(1)} %collective-permute-done.2.v3) | copy-start | bytes 221188
  10.1 1.0 copy-start.22
  11.1 0.6 copy-start.23
  16.7 3.1 %collective-permute-start.3 = (bf16[16,16,2304]{2,1,0:T(8,128)(2,1)}, bf16[16,16,2304]{2,1,0:T(8,128)(2,1)S(1)}, u32[]{:S(2)}, u32[]{:S(2)}) collective-permute-start(bf16[16,16,2304]{2,1,0:T(8,128)(2,1)} %get-tuple-element.9), channel_id=1, source_target_pairs={{0,4},{4,0},{8,12},{12,8},{16,20},{20,16},{24,28},{28,24},{32,36},... | collective-permute-start | bytes 3538952 | tf_op jit(solution)/shard_map/ppermute | solution.py:230
  18.1 1.8 %copy-start.18 = (bf16[2,16,2304]{2,1,0:T(8,128)(2,1)S(1)}, bf16[2,16,2304]{2,1,0:T(8,128)(2,1)}, u32[]{:S(2)}) copy-start(bf16[2,16,2304]{2,1,0:T(8,128)(2,1)} %get-tuple-element.10) | copy-start | bytes 442372
  20.0 16.0 %copy-start.8 = (bf16[4,16,2304]{2,1,0:T(8,128)(2,1)}, bf16[4,16,2304]{2,1,0:T(8,128)(2,1)S(1)}, u32[]{:S(2)}) copy-start(bf16[4,16,2304]{2,1,0:T(8,128)(2,1)S(1)} %pad_maximum_fusion.7.refs_2_) | copy-start | bytes 884740
  20.0 10.3 %collective-permute-start.10 = (bf16[4,16,2304]{2,1,0:T(8,128)(2,1)S(1)}, bf16[4,16,2304]{2,1,0:T(8,128)(2,1)S(1)}, u32[]{:S(2)}, u32[]{:S(2)}) collective-permute-start(bf16[4,16,2304]{2,1,0:T(8,128)(2,1)S(1)} %pad_maximum_fusion.7.refs_2_), channel_id=1, source_target_pairs={{0,192},{64,0},{128,64},{192,128},{1,193},{65,1},{129,65},{193,129... | collective-permute-start | bytes 884744 | tf_op jit(solution)/shard_map/ppermute | solution.py:199
  20.9 9.5 %collective-permute-start.9 = (bf16[4,16,2304]{2,1,0:T(8,128)(2,1)S(1)}, bf16[4,16,2304]{2,1,0:T(8,128)(2,1)S(1)}, u32[]{:S(2)}, u32[]{:S(2)}) collective-permute-start(bf16[4,16,2304]{2,1,0:T(8,128)(2,1)S(1)} %pad_maximum_fusion.7.refs_2_), channel_id=1, source_target_pairs={{0,64},{64,128},{128,192},{192,0},{1,65},{65,129},{129,193},{193,1... | collective-permute-start | bytes 884744 | tf_op jit(solution)/shard_map/ppermute | solution.py:199
  23.3 12.7 %collective-permute-start.11 = (bf16[4,16,2304]{2,1,0:T(8,128)(2,1)S(1)}, bf16[4,16,2304]{2,1,0:T(8,128)(2,1)S(1)}, u32[]{:S(2)}, u32[]{:S(2)}) collective-permute-start(bf16[4,16,2304]{2,1,0:T(8,128)(2,1)S(1)} %pad_maximum_fusion.8), channel_id=1, source_target_pairs={{0,8},{4,12},{8,16},{12,20},{16,24},{20,28},{24,32},{28,36},{32,40... | collective-permute-start | bytes 884744 | tf_op jit(solution)/shard_map/ppermute | solution.py:199
  25.3 10.7 %collective-permute-start.12 = (bf16[4,16,2304]{2,1,0:T(8,128)(2,1)S(1)}, bf16[4,16,2304]{2,1,0:T(8,128)(2,1)S(1)}, u32[]{:S(2)}, u32[]{:S(2)}) collective-permute-start(bf16[4,16,2304]{2,1,0:T(8,128)(2,1)S(1)} %pad_maximum_fusion.9), channel_id=1, source_target_pairs={{0,56},{4,60},{8,0},{12,4},{16,8},{20,12},{24,16},{28,20},{32,24},... | collective-permute-start | bytes 884744 | tf_op jit(solution)/shard_map/ppermute | solution.py:199
  30.3 5.7 %copy-start.11 = (bf16[4,16,2304]{2,1,0:T(8,128)(2,1)}, bf16[4,16,2304]{2,1,0:T(8,128)(2,1)S(1)}, u32[]{:S(2)}) copy-start(bf16[4,16,2304]{2,1,0:T(8,128)(2,1)S(1)} %collective-permute-done.10.refs_1_) | copy-start | bytes 884740
  30.3 5.7 %copy-start.12 = (bf16[4,16,2304]{2,1,0:T(8,128)(2,1)}, bf16[4,16,2304]{2,1,0:T(8,128)(2,1)S(1)}, u32[]{:S(2)}) copy-start(bf16[4,16,2304]{2,1,0:T(8,128)(2,1)S(1)} %collective-permute-done.9.refs_0_) | copy-start | bytes 884740
  36.0 0.7 copy-start.4
  36.0 0.8 copy-start.5
  36.8 18.6 %collective-permute-start.14 = (bf16[10,16,2304]{2,1,0:T(8,128)(2,1)S(1)}, bf16[10,16,2304]{2,1,0:T(8,128)(2,1)S(1)}, u32[]{:S(2)}, u32[]{:S(2)}) collective-permute-start(bf16[10,16,2304]{2,1,0:T(8,128)(2,1)S(1)} %get-tuple-element.30), channel_id=1, source_target_pairs={{0,192},{64,0},{128,64},{192,128},{1,193},{65,1},{129,65},{193,129... | collective-permute-start | bytes 2211848 | tf_op jit(solution)/shard_map/ppermute | solution.py:199
  36.9 18.6 %collective-permute-start.13 = (bf16[10,16,2304]{2,1,0:T(8,128)(2,1)S(1)}, bf16[10,16,2304]{2,1,0:T(8,128)(2,1)S(1)}, u32[]{:S(2)}, u32[]{:S(2)}) collective-permute-start(bf16[10,16,2304]{2,1,0:T(8,128)(2,1)S(1)} %get-tuple-element.31), channel_id=1, source_target_pairs={{0,64},{64,128},{128,192},{192,0},{1,65},{65,129},{129,193},{193,1... | collective-permute-start | bytes 2211848 | tf_op jit(solution)/shard_map/ppermute | solution.py:199
  40.1 21.9 %collective-permute-start.15 = (bf16[4,16,2304]{2,1,0:T(8,128)(2,1)S(1)}, bf16[4,16,2304]{2,1,0:T(8,128)(2,1)S(1)}, u32[]{:S(2)}, u32[]{:S(2)}) collective-permute-start(bf16[4,16,2304]{2,1,0:T(8,128)(2,1)S(1)} %pad_maximum_fusion.10), channel_id=1, source_target_pairs={{0,16},{4,20},{8,24},{12,28},{16,32},{20,36},{24,40},{28,44},{32,4... | collective-permute-start | bytes 884744 | tf_op jit(solution)/shard_map/ppermute | solution.py:199
  42.4 19.6 %collective-permute-start.16 = (bf16[4,16,2304]{2,1,0:T(8,128)(2,1)S(1)}, bf16[4,16,2304]{2,1,0:T(8,128)(2,1)S(1)}, u32[]{:S(2)}, u32[]{:S(2)}) collective-permute-start(bf16[4,16,2304]{2,1,0:T(8,128)(2,1)S(1)} %pad_maximum_fusion.11), channel_id=1, source_target_pairs={{0,48},{4,52},{8,56},{12,60},{16,0},{20,4},{24,8},{28,12},{32,16},... | collective-permute-start | bytes 884744 | tf_op jit(solution)/shard_map/ppermute | solution.py:199
  44.5 45.2 %collective-permute-start.4 = (bf16[4,16,2304]{2,1,0:T(8,128)(2,1)S(1)}, bf16[4,16,2304]{2,1,0:T(8,128)(2,1)}, u32[]{:S(2)}, u32[]{:S(2)}) collective-permute-start(bf16[4,16,2304]{2,1,0:T(8,128)(2,1)S(1)} %pad_maximum_fusion.6), channel_id=1, source_target_pairs={{0,32},{4,36},{8,40},{12,44},{16,48},{20,52},{24,56},{28,60},{32,0... | collective-permute-start | bytes 884744 | tf_op jit(solution)/shard_map/ppermute | solution.py:199
  55.4 6.8 %copy-start.2 = (bf16[10,16,2304]{2,1,0:T(8,128)(2,1)}, bf16[10,16,2304]{2,1,0:T(8,128)(2,1)S(1)}, u32[]{:S(2)}) copy-start(bf16[10,16,2304]{2,1,0:T(8,128)(2,1)S(1)} %collective-permute-done.14.refs_4_) | copy-start | bytes 2211844
  55.5 6.7 %copy-start.3 = (bf16[10,16,2304]{2,1,0:T(8,128)(2,1)}, bf16[10,16,2304]{2,1,0:T(8,128)(2,1)S(1)}, u32[]{:S(2)}) copy-start(bf16[10,16,2304]{2,1,0:T(8,128)(2,1)S(1)} %collective-permute-done.13.refs_3_) | copy-start | bytes 2211844
  62.0 0.7 copy-start.6
  62.0 0.8 copy-start.7
  62.8 26.2 %copy-start.20 = (s32[16,16]{1,0:T(8,128)S(1)}, s32[16,16]{1,0:T(8,128)}, u32[]{:S(2)}) copy-start(s32[16,16]{1,0:T(8,128)} %param.11) | copy-start | bytes 3076
  62.8 35.3 %collective-permute-start.18 = (bf16[12,16,2304]{2,1,0:T(8,128)(2,1)S(1)}, bf16[12,16,2304]{2,1,0:T(8,128)(2,1)S(1)}, u32[]{:S(2)}, u32[]{:S(2)}) collective-permute-start(bf16[12,16,2304]{2,1,0:T(8,128)(2,1)S(1)} %get-tuple-element.28), channel_id=1, source_target_pairs={{0,192},{64,0},{128,64},{192,128},{1,193},{65,1},{129,65},{193,129... | collective-permute-start | bytes 2654216 | tf_op jit(solution)/shard_map/ppermute | solution.py:199
  62.9 25.3 %collective-permute-start.19 = (bf16[4,16,2304]{2,1,0:T(8,128)(2,1)S(1)}, bf16[4,16,2304]{2,1,0:T(8,128)(2,1)S(1)}, u32[]{:S(2)}, u32[]{:S(2)}) collective-permute-start(bf16[4,16,2304]{2,1,0:T(8,128)(2,1)S(1)} %pad_maximum_fusion.12), channel_id=1, source_target_pairs={{0,24},{4,28},{8,32},{12,36},{16,40},{20,44},{24,48},{28,52},{32,5... | collective-permute-start | bytes 884744 | tf_op jit(solution)/shard_map/ppermute | solution.py:199
  74.6 27.7 %collective-permute-start.17 = (bf16[12,16,2304]{2,1,0:T(8,128)(2,1)S(1)}, bf16[12,16,2304]{2,1,0:T(8,128)(2,1)S(1)}, u32[]{:S(2)}, u32[]{:S(2)}) collective-permute-start(bf16[12,16,2304]{2,1,0:T(8,128)(2,1)S(1)} %get-tuple-element.29), channel_id=1, source_target_pairs={{0,64},{64,128},{128,192},{192,0},{1,65},{65,129},{129,193},{193,1... | collective-permute-start | bytes 2654216 | tf_op jit(solution)/shard_map/ppermute | solution.py:199
  77.9 13.1 %collective-permute-start.21 = (bf16[4,16,2304]{2,1,0:T(8,128)(2,1)S(1)}, bf16[4,16,2304]{2,1,0:T(8,128)(2,1)S(1)}, u32[]{:S(2)}, u32[]{:S(2)}) collective-permute-start(bf16[4,16,2304]{2,1,0:T(8,128)(2,1)S(1)} %pad_maximum_fusion.13), channel_id=1, source_target_pairs={{0,40},{4,44},{8,48},{12,52},{16,56},{20,60},{24,0},{28,4},{32,8},... | collective-permute-start | bytes 884744 | tf_op jit(solution)/shard_map/ppermute | solution.py:199
  88.2 14.2 %copy-start.9 = (bf16[4,16,2304]{2,1,0:T(8,128)(2,1)}, bf16[4,16,2304]{2,1,0:T(8,128)(2,1)S(1)}, u32[]{:S(2)}) copy-start(bf16[4,16,2304]{2,1,0:T(8,128)(2,1)S(1)} %collective-permute-done.19.refs_15_) | copy-start | bytes 884740
  88.2 10.0 %collective-permute-start.20 = (bf16[4,16,2304]{2,1,0:T(8,128)(2,1)S(1)}, bf16[4,16,2304]{2,1,0:T(8,128)(2,1)}, u32[]{:S(2)}, u32[]{:S(2)}) collective-permute-start(bf16[4,16,2304]{2,1,0:T(8,128)(2,1)S(1)} %collective-permute-done.19.refs_15_), channel_id=1, source_target_pairs={{0,64},{64,128},{128,192},{192,0},{1,65},{65,129},{129,193},{193,1... | collective-permute-start | bytes 884744 | tf_op jit(solution)/shard_map/ppermute | solution.py:199
  89.7 13.7 %collective-permute-start.7 = (bf16[4,16,2304]{2,1,0:T(8,128)(2,1)}, bf16[4,16,2304]{2,1,0:T(8,128)(2,1)S(1)}, u32[]{:S(2)}, u32[]{:S(2)}) collective-permute-start(bf16[4,16,2304]{2,1,0:T(8,128)(2,1)} %collective-permute-done.4.refs_21_), channel_id=1, source_target_pairs={{0,192},{64,0},{128,64},{192,128},{1,193},{65,1},{129,65},{193,129... | collective-permute-start | bytes 884744 | tf_op jit(solution)/shard_map/ppermute | solution.py:199
  90.9 11.4 %copy-start.10 = (bf16[4,16,2304]{2,1,0:T(8,128)(2,1)}, bf16[4,16,2304]{2,1,0:T(8,128)(2,1)S(1)}, u32[]{:S(2)}) copy-start(bf16[4,16,2304]{2,1,0:T(8,128)(2,1)S(1)} %collective-permute-done.21.refs_16_) | copy-start | bytes 884740
  90.9 16.0 %collective-permute-start.5 = (bf16[4,16,2304]{2,1,0:T(8,128)(2,1)}, bf16[4,16,2304]{2,1,0:T(8,128)(2,1)S(1)}, u32[]{:S(2)}, u32[]{:S(2)}) collective-permute-start(bf16[4,16,2304]{2,1,0:T(8,128)(2,1)} %collective-permute-done.4.refs_21_), channel_id=1, source_target_pairs={{0,64},{64,128},{128,192},{192,0},{1,65},{65,129},{129,193},{193,1... | collective-permute-start | bytes 884744 | tf_op jit(solution)/shard_map/ppermute | solution.py:199
  98.2 10.9 %collective-permute-start.23 = (bf16[4,16,2304]{2,1,0:T(8,128)(2,1)S(1)}, bf16[4,16,2304]{2,1,0:T(8,128)(2,1)}, u32[]{:S(2)}, u32[]{:S(2)}) collective-permute-start(bf16[4,16,2304]{2,1,0:T(8,128)(2,1)S(1)} %collective-permute-done.21.refs_16_), channel_id=1, source_target_pairs={{0,192},{64,0},{128,64},{192,128},{1,193},{65,1},{129,65},{193,129... | collective-permute-start | bytes 884744 | tf_op jit(solution)/shard_map/ppermute | solution.py:199
  98.2 4.2 %copy-start = (bf16[12,16,2304]{2,1,0:T(8,128)(2,1)}, bf16[12,16,2304]{2,1,0:T(8,128)(2,1)S(1)}, u32[]{:S(2)}) copy-start(bf16[12,16,2304]{2,1,0:T(8,128)(2,1)S(1)} %collective-permute-done.18.refs_8_) | copy-start | bytes 2654212
  98.2 12.6 %collective-permute-start.25 = (bf16[4,16,2304]{2,1,0:T(8,128)(2,1)}, bf16[4,16,2304]{2,1,0:T(8,128)(2,1)}, u32[]{:S(2)}, u32[]{:S(2)}) collective-permute-start(bf16[4,16,2304]{2,1,0:T(8,128)(2,1)} %collective-permute-done.20.refs_11_), channel_id=1, source_target_pairs={{0,64},{64,128},{128,192},{192,0},{1,65},{65,129},{129,193},{193,1... | collective-permute-start | bytes 884744 | tf_op jit(solution)/shard_map/ppermute | solution.py:199
  102.3 4.7 %copy-start.1 = (bf16[12,16,2304]{2,1,0:T(8,128)(2,1)}, bf16[12,16,2304]{2,1,0:T(8,128)(2,1)S(1)}, u32[]{:S(2)}) copy-start(bf16[12,16,2304]{2,1,0:T(8,128)(2,1)S(1)} %collective-permute-done.17.refs_7_) | copy-start | bytes 2654212
  102.3 26.3 %collective-permute-start.24 = (bf16[8,16,2304]{2,1,0:T(8,128)(2,1)}, bf16[8,16,2304]{2,1,0:T(8,128)(2,1)S(1)}, u32[]{:S(2)}, u32[]{:S(2)}) collective-permute-start(bf16[8,16,2304]{2,1,0:T(8,128)(2,1)} %pad_maximum_fusion.5), channel_id=1, source_target_pairs={{0,192},{64,0},{128,64},{192,128},{1,193},{65,1},{129,65},{193,129... | collective-permute-start | bytes 1769480 | tf_op jit(solution)/shard_map/ppermute | solution.py:199
  103.4 25.2 %copy-start.13 = (bf16[4,16,2304]{2,1,0:T(8,128)(2,1)}, bf16[4,16,2304]{2,1,0:T(8,128)(2,1)S(1)}, u32[]{:S(2)}) copy-start(bf16[4,16,2304]{2,1,0:T(8,128)(2,1)S(1)} %collective-permute-done.7.refs_19_) | copy-start | bytes 884740
  103.4 25.2 %collective-permute-start.22 = (bf16[8,16,2304]{2,1,0:T(8,128)(2,1)}, bf16[8,16,2304]{2,1,0:T(8,128)(2,1)S(1)}, u32[]{:S(2)}, u32[]{:S(2)}) collective-permute-start(bf16[8,16,2304]{2,1,0:T(8,128)(2,1)} %pad_maximum_fusion.4), channel_id=1, source_target_pairs={{0,64},{64,128},{128,192},{192,0},{1,65},{65,129},{129,193},{193,1... | collective-permute-start | bytes 1769480 | tf_op jit(solution)/shard_map/ppermute | solution.py:199
  106.9 21.7 %copy-start.14 = (bf16[4,16,2304]{2,1,0:T(8,128)(2,1)}, bf16[4,16,2304]{2,1,0:T(8,128)(2,1)S(1)}, u32[]{:S(2)}) copy-start(bf16[4,16,2304]{2,1,0:T(8,128)(2,1)S(1)} %collective-permute-done.5.refs_17_) | copy-start | bytes 884740
  106.9 32.5 %collective-permute-start.8 = (bf16[2,16,2304]{2,1,0:T(8,128)(2,1)S(1)}, bf16[2,16,2304]{2,1,0:T(8,128)(2,1)}, u32[]{:S(2)}, u32[]{:S(2)}) collective-permute-start(bf16[2,16,2304]{2,1,0:T(8,128)(2,1)S(1)} %slice.94), channel_id=1, source_target_pairs={{0,192},{64,0},{128,64},{192,128},{1,193},{65,1},{129,65},{193,129... | collective-permute-start | bytes 442376 | tf_op jit(solution)/shard_map/ppermute | solution.py:199
  109.1 30.4 %collective-permute-start.6 = (bf16[2,16,2304]{2,1,0:T(8,128)(2,1)S(1)}, bf16[2,16,2304]{2,1,0:T(8,128)(2,1)S(1)}, u32[]{:S(2)}, u32[]{:S(2)}) collective-permute-start(bf16[2,16,2304]{2,1,0:T(8,128)(2,1)S(1)} %slice.93), channel_id=1, source_target_pairs={{0,64},{64,128},{128,192},{192,0},{1,65},{65,129},{129,193},{193,1... | collective-permute-start | bytes 442376 | tf_op jit(solution)/shard_map/ppermute | solution.py:199
  110.8 17.8 %collective-permute-start.26 = (bf16[4,16,2304]{2,1,0:T(8,128)(2,1)}, bf16[4,16,2304]{2,1,0:T(8,128)(2,1)S(1)}, u32[]{:S(2)}, u32[]{:S(2)}) collective-permute-start(bf16[4,16,2304]{2,1,0:T(8,128)(2,1)} %collective-permute-done.23.refs_13_), channel_id=1, source_target_pairs={{0,192},{64,0},{128,64},{192,128},{1,193},{65,1},{129,65},{193,129... | collective-permute-start | bytes 884744 | tf_op jit(solution)/shard_map/ppermute | solution.py:199
  128.6 0.7 copy-start.17
  128.6 0.9 copy-start.15
  128.6 1.1 copy-start.16
  139.5 0.6 copy-start.19
where the time goes:
time: 142 us
  waiting for transfers between devices  60.3 us (42%)
  starting transfers between devices  53 us (37%)
  Pallas kernels  16.4 us (12%)
  local copies, waits for them, and re-layouts  6.73 us (5%)
  other arithmetic  4.88 us (3%)
    ppermute x26, waiting for transfers between devices, shift(): lax.ppermute(value, axis, [(i, (i + by) % size) for i in range(size)])  58.6 us
    ppermute x26, starting transfers between devices, shift(): lax.ppermute(value, axis, [(i, (i + by) % size) for i in range(size)])  52.9 us
    pallas_call x2, Pallas kernels, place(): pl.pallas_call(functools.partial(place_kernel, pieces, first), out_shape=...  11.5 us
    pallas_call x1, Pallas kernels, merge(): pl.pallas_call(merge_kernel, out_shape=[slots(PAIR), slots(16 - PAIR), sl...  4.94 us
    unnamed x48, local copies, waits for them, and re-layouts  3.67 us
  transfers between devices with their start and end apart: 27, of which 13 were waited for; matrix products, arithmetic and copies ran while one was open for 5% of the time, Pallas kernels for 7%

commit v1 on v0

--- a/solution.py
+++ b/solution.py
@@ -25,34 +25,71 @@
     return lax.dot_general(a, b, (((0,), (0,)), ((), ())), preferred_element_type=jnp.float32)
 
 
+def weave_kernel(gate_hbm, up_hbm, down_hbm, woven_ref, gate_ref, up_ref, sems):
+    rows, hidden = gate_ref.shape
+    loads = [
+        pltpu.make_async_copy(gate_hbm, gate_ref, sems.at[0]),
+        pltpu.make_async_copy(up_hbm, up_ref, sems.at[1]),
+        pltpu.make_async_copy(down_hbm, woven_ref.at[:, pl.ds(2 * hidden, hidden)], sems.at[2]),
+    ]
+    for load in loads:
+        load.start()
+    half = 128
+    spread = selector(
+        2 * half, 2 * half, lambda row: jnp.where(row < half, 2 * row, 2 * (row - half) + 1)
+    )
+    loads[0].wait()
+    loads[1].wait()
+    for block in range(hidden // half):
+        src = slice(block * half, (block + 1) * half)
+        dst = slice(2 * block * half, 2 * (block + 1) * half)
+        both = jnp.concatenate([gate_ref[:, src], up_ref[:, src]], axis=1)
+        woven_ref[:, dst] = dot(both, spread).astype(jnp.bfloat16)
+    loads[2].wait()
+
+
+def weave(gate, up, down):
+    rows, hidden = gate.shape
+    return pl.pallas_call(
+        weave_kernel,
+        out_shape=jax.ShapeDtypeStruct((rows, 3 * hidden), jnp.bfloat16),
+        in_specs=[pl.BlockSpec(memory_space=pl.ANY)] * 3,
+        out_specs=pl.BlockSpec(memory_space=pltpu.VMEM),
+        scratch_shapes=[
+            pltpu.VMEM((rows, hidden), jnp.bfloat16),
+            pltpu.VMEM((rows, hidden), jnp.bfloat16),
+            pltpu.SemaphoreType.DMA((3,)),
+        ],
+        compiler_params=pltpu.CompilerParams(vmem_limit_bytes=8 << 20),
+        cost_estimate=pl.CostEstimate(
+            flops=2 * rows * hidden * 512, bytes_accessed=2_400_000, transcendentals=0
+        ),
+    )(gate, up, down)
+
+
 def merge_kernel(
-    index_ref, tensor_ref, gate_hbm, up_hbm, down_hbm, width_hbm, v0, v1, v2, v3,
-    self_ref, keep_ref, swap_ref, mixed_ref, plain_ref, merged_ref,
-    gate_ref, up_ref, down_ref, width_ref, parts_ref, sems,
+    index_ref, tensor_ref, woven_ref, width_hbm, own_hbm, v1, v2, v3,
+    self_ref, keep_ref, swap_ref, mixed_ref, plain_ref, merged_ref, width_ref, own_ref, sems,
 ):
-    parts = [parts_ref.at[j] for j in range(4)]
     loads = [
-        pltpu.make_async_copy(src, dst, sems.at[j])
-        for j, (src, dst) in enumerate(
-            zip(
-                (v0, v1, v2, v3, gate_hbm, up_hbm, width_hbm, down_hbm),
-                (*parts, gate_ref, up_ref, width_ref, down_ref),
-            )
-        )
+        pltpu.make_async_copy(own_hbm, own_ref, sems.at[0]),
+        pltpu.make_async_copy(width_hbm, width_ref, sems.at[1]),
     ]
     for load in loads:
         load.start()
     slabs = index_ref.shape[0]
-    rows, hidden = gate_ref.shape
+    rows, wide = woven_ref.shape
+    hidden = wide // 3
     slab_rows = rows // slabs
     rank = width_ref.shape[1]
-    part = parts_ref.shape[3]
+    part = own_ref.shape[2]
     me = tensor_ref[0]
     even = selector(part, 2 * part, lambda row: 2 * row)
     odd = selector(part, 2 * part, lambda row: 2 * row + 1)
     plain_ref[...] = jnp.zeros_like(plain_ref)
-    for j, v in enumerate(parts):
-        loads[j].wait()
+    for j, v in ((1, v1), (2, v2), (3, v3), (0, own_ref)):
+        if j == 0:
+            loads[0].wait()
         home = lax.rem(me - j + 4, 4)
         cols = pl.ds(pl.multiple_of(home * (2 * part), 128), 2 * part)
         mixed_ref[:rank, cols] = dot(v[0], even).astype(jnp.bfloat16)
@@ -60,22 +97,17 @@
         shift = lax.rem(home, 2) * part
         pair_cols = pl.ds(pl.multiple_of(lax.div(home, 2) * (2 * part), 128), 2 * part)
         plain_ref[:, pair_cols] += dot(v[2], selector(part, 2 * part, lambda row: row + shift))
-    half = 128
-    spread = selector(
-        2 * half, 2 * half, lambda row: jnp.where(row < half, 2 * row, 2 * (row - half) + 1)
-    )
-    for load in loads[4:]:
-        load.wait()
+    loads[1].wait()
     both = width_ref[0:2].reshape(2 * rank, rows)
-    for block in range(hidden // half):
-        src = slice(block * half, (block + 1) * half)
-        dst = slice(2 * block * half, 2 * (block + 1) * half)
-        weight = dot(jnp.concatenate([gate_ref[:, src], up_ref[:, src]], axis=1), spread)
+    for block in range(2 * hidden // 256):
+        dst = slice(block * 256, (block + 1) * 256)
         delta = dot_t(both, mixed_ref[:, dst])
-        merged_ref[:, dst] = (weight + ADAPTER_SCALE * delta).astype(jnp.bfloat16)
+        merged_ref[:, dst] = (
+            woven_ref[:, dst].astype(jnp.float32) + ADAPTER_SCALE * delta
+        ).astype(jnp.bfloat16)
     delta = dot_t(width_ref[2], plain_ref[...].astype(jnp.bfloat16))
     merged_ref[:, 2 * hidden :] = (
-        down_ref[...].astype(jnp.float32) + ADAPTER_SCALE * delta
+        woven_ref[:, 2 * hidden :].astype(jnp.float32) + ADAPTER_SCALE * delta
     ).astype(jnp.bfloat16)
     bucket = swap_ref.shape[0]
     for k in range(slabs):
@@ -95,11 +127,10 @@
             swap_ref[index - bucket] = merged_ref[block, :]
 
 
-def merge(index, tensor, gate, up, down, width, parts):
-    rows, hidden = gate.shape
+def merge(index, tensor, woven, width, parts):
+    rows, wide = woven.shape
     rank = width.shape[1]
     slab_rows = rows // index.shape[0]
-    wide = 3 * hidden
     smem = pl.BlockSpec(memory_space=pltpu.SMEM)
     vmem = pl.BlockSpec(memory_space=pltpu.VMEM)
 
@@ -109,56 +140,65 @@
     return pl.pallas_call(
         merge_kernel,
         out_shape=[slots(PAIR), slots(16 - PAIR), slots(16)],
-        in_specs=[smem, smem] + [pl.BlockSpec(memory_space=pl.ANY)] * 8,
+        in_specs=[smem, smem, vmem] + [pl.BlockSpec(memory_space=pl.ANY)] * 2 + [vmem] * 3,
         out_specs=[vmem] * 3,
         scratch_shapes=[
-            pltpu.VMEM((2 * rank, 2 * hidden), jnp.bfloat16),
-            pltpu.VMEM((rank, hidden), jnp.float32),
+            pltpu.VMEM((2 * rank, 2 * wide // 3), jnp.bfloat16),
+            pltpu.VMEM((rank, wide // 3), jnp.float32),
             pltpu.VMEM((rows, wide), jnp.bfloat16),
-            pltpu.VMEM((rows, hidden), jnp.bfloat16),
-            pltpu.VMEM((rows, hidden), jnp.bfloat16),
-            pltpu.VMEM((rows, hidden), jnp.bfloat16),
             pltpu.VMEM(width.shape, jnp.bfloat16),
-            pltpu.VMEM((4, *parts[0].shape), jnp.bfloat16),
-            pltpu.SemaphoreType.DMA((8,)),
+            pltpu.VMEM(parts[0].shape, jnp.bfloat16),
+            pltpu.SemaphoreType.DMA((2,)),
         ],
+        compiler_params=pltpu.CompilerParams(vmem_limit_bytes=12 << 20),
         cost_estimate=pl.CostEstimate(
-            flops=2 * rows * wide * 384, bytes_accessed=4_000_000, transcendentals=0
+            flops=2 * rows * wide * 128, bytes_accessed=4_000_000, transcendentals=0
         ),
-    )(index, tensor, gate, up, down, width, *parts)
-
-
-def place_kernel(pieces, first, dest_ref, count_ref, relay_ref, *refs):
-    if first:
-        bufs, (out_ref, sems, zero_ref, zero_sems) = refs[:-4], refs[-4:]
-    else:
-        bufs, (_, out_ref, sems) = refs[:-3], refs[-3:]
+    )(index, tensor, woven, width, *parts)
+
+
+def place_kernel(pieces, count, first, dest_ref, count_ref, relay_ref, *refs):
+    bufs, refs = refs[:count], refs[count if first else count + 1 :]
+    out_ref, refs = refs[0], refs[1:]
+    held, refs = refs[:count], refs[count:]
+    load_sems, sems = refs[:2]
     groups = out_ref.shape[1]
+    loads = [pltpu.make_async_copy(bufs[j], held[j], load_sems.at[j]) for j in range(count)]
+    for load in loads:
+        load.start()
 
     def copy(number):
         which, row, entry, shift = pieces[number]
         group = lax.rem(relay_ref[0] + shift, groups)
         dest = jnp.maximum(dest_ref[entry], 0)
         return pltpu.make_async_copy(
-            bufs[which].at[row], out_ref.at[dest, group, 0], sems.at[number]
+            held[which].at[row], out_ref.at[dest, group, 0], sems.at[number]
         )
 
-    def blank(slot):
-        return pltpu.make_async_copy(zero_ref, out_ref.at[slot], zero_sems.at[slot])
-
-    for number, piece in enumerate(pieces):
-
-        @pl.when(dest_ref[piece[2]] >= 0)
-        def _():
-            copy(number).start()
-
     if first:
+        zero_ref, zero_sems = refs[2:]
+
+        def blank(slot):
+            return pltpu.make_async_copy(zero_ref, out_ref.at[slot], zero_sems.at[slot])
+
         zero_ref[...] = jnp.zeros_like(zero_ref)
 
         @pl.loop(count_ref[0], out_ref.shape[0])
         def _(slot):
             blank(slot).start()
 
+    ready = set()
+    for number, piece in enumerate(pieces):
+        if piece[0] not in ready:
+            ready.add(piece[0])
+            loads[piece[0]].wait()
+
+        @pl.when(dest_ref[piece[2]] >= 0)
+        def _():
+            copy(number).start()
+
+    if first:
+
         @pl.loop(count_ref[0], out_ref.shape[0])
         def _(slot):
             blank(slot).wait()
@@ -170,28 +210,30 @@
             copy(number).wait()
 
 
-def place(out, pieces, dest, count, relay, bufs, out_shape):
+def place(out, pieces, dest, total, relay, bufs, out_shape):
     smem = pl.BlockSpec(memory_space=pltpu.SMEM)
-    vmem = pl.BlockSpec(memory_space=pltpu.VMEM)
     anywhere = pl.BlockSpec(memory_space=pl.ANY)
     first = out is None
-    scratch = [pltpu.SemaphoreType.DMA((len(pieces),))]
+    count = len(bufs)
+    pieces = sorted(pieces)
+    scratch = [pltpu.VMEM(buf.shape, jnp.bfloat16) for buf in bufs]
+    scratch += [pltpu.SemaphoreType.DMA((count,)), pltpu.SemaphoreType.DMA((len(pieces),))]
     if first:
         scratch += [
             pltpu.VMEM(out_shape[1:], jnp.bfloat16),
             pltpu.SemaphoreType.DMA((out_shape[0],)),
         ]
     return pl.pallas_call(
-        functools.partial(place_kernel, pieces, first),
+        functools.partial(place_kernel, pieces, count, first),
         out_shape=jax.ShapeDtypeStruct(out_shape, jnp.bfloat16),
-        in_specs=[smem] * 3 + [vmem] * len(bufs) + ([] if first else [anywhere]),
+        in_specs=[smem] * 3 + [anywhere] * (count if first else count + 1),
         out_specs=anywhere,
         scratch_shapes=scratch,
-        input_output_aliases={} if first else {3 + len(bufs): 0},
+        input_output_aliases={} if first else {3 + count: 0},
         cost_estimate=pl.CostEstimate(
-            flops=0, bytes_accessed=len(pieces) * 73728, transcendentals=0
+            flops=0, bytes_accessed=2 * len(pieces) * 73728, transcendentals=0
         ),
-    )(dest, count, relay, *bufs, *([] if first else [out]))
+    )(dest, total, relay, *bufs, *([] if first else [out]))
 
 
 def shift(value, axis, by):
@@ -222,7 +264,7 @@
     own, keep, swap = merge(
         index,
         lax.axis_index("tensor").astype(jnp.int32)[None],
-        gate[0], up[0], down[0],
+        weave(gate[0], up[0], down[0]),
         jnp.swapaxes(width[0], 1, 2),
         parts,
     )
@@ -241,10 +283,9 @@
     steps = [
         ([0], [near], False, False),
         ([1, chips - 1], None, False, False),
-        ([2, chips - 2], None, False, False),
-        ([3, chips - 3], None, True, False),
+        ([2, chips - 2], None, False, True),
+        ([3, chips - 3], None, False, False),
         ([4], None, True, True),
-        ([], [], False, True),
     ]
     sources = jnp.stack(
         [((me - 2 * d) % owners) ^ core for names, *_ in steps for d in names for core in (0, 1)]
@@ -300,6 +341,9 @@
                 (*from_right[j], where[turned[j]], 1),
             ]
         earlier = [base + j for j in range(count)]
+        if names == [4]:
+            across = ring([items], 2)
+            pieces += [(*across[j], base + j, 2) for j in range(count)]
         entry += count
         half = count // 2
         forward_right = forward_left = []

time: 142 us -> 132 us (0.930)
  the two profiles are of different devices: /device:TPU:6 before, /device:TPU:32 now
where the time goes in v1:
time: 132 us; the launch traced here: 131 us
  waiting for transfers between devices  65.4 us (50%)
  starting transfers between devices  37.5 us (28%)
  Pallas kernels  15.8 us (12%)
  local copies, waits for them, and re-layouts  8.6 us (7%)
  other arithmetic  3.56 us (3%)
    ppermute x23, waiting for transfers between devices, shift(): lax.ppermute(value, axis, [(i, (i + by) % size) for i in range(size)])  63.3 us
    ppermute x23, starting transfers between devices, shift(): lax.ppermute(value, axis, [(i, (i + by) % size) for i in range(size)])  37.5 us
    pallas_call x2, Pallas kernels, place(): pl.pallas_call(functools.partial(place_kernel, pieces, count, first), out...  12.6 us
    unnamed x50, local copies, waits for them, and re-layouts  5.48 us
  transfers between devices with their start and end apart: 24, of which 15 were waited for; matrix products, arithmetic and copies ran while one was open for 3% of the time, Pallas kernels for 7%

profile of v1, /device:TPU:32, one launch (start us, length us, event | category | flops | bytes accessed | tf_op | source)
XLA Modules:
  0.0 131.4 jit_solution(7314839909578717444)
XLA Ops:
  0.0 3.0 %collective-permute-start.2 = (bf16[3,64,192]{2,1,0:T(8,128)(2,1)}, bf16[3,64,192]{2,1,0:T(8,128)(2,1)S(1)}, u32[]{:S(2)}, u32[]{:S(2)}) collective-permute-start(bf16[3,64,192]{2,1,0:T(8,128)(2,1)} %bitcast.34), channel_id=1, source_target_pairs={{0,3},{1,0},{2,1},{3,2},{4,7},{5,4},{6,5},{7,6},{8,11},{9,8},{10,9... | collective-permute-start | bytes 221192 | tf_op jit(solution)/shard_map/ppermute | solution.py:241
  3.0 0.6 collective-permute-start.1
  3.6 1.0 collective-permute-start
  4.6 0.7 dynamic-slice_bitcast_fusion
  5.3 0.2 convert_reduce_fusion.2
  5.5 0.7 fusion.3.index_ref
  6.2 1.0 copy-done
  7.2 1.0 copy-done.1
  8.2 1.0 copy-done.2
  9.2 0.8 shard_map.64.woven_ref
  10.0 0.0 collective-permute-done.1.v2
  10.1 1.0 collective-permute-done.v1
  11.1 2.3 %shard_map.65 = (bf16[2,16,2304]{2,1,0:T(8,128)(2,1)S(1)}, bf16[14,16,2304]{2,1,0:T(8,128)(2,1)S(1)}, bf16[16,16,2304]{2,1,0:T(8,128)(2,1)S(1)}) custom-call(s32[16]{0:T(128)S(1)} %fusion.3.index_ref, s32[1]{0:T(128)} %bitcast.19.tensor_ref, bf16[256,2304]{1,0:T(8,128)(2,1)S(1)} %shard_map.64.woven_ref, bf16[3,64,256]{2,1,0:T(8,128)(2,1)S(1)} %bitcast.33, ...), custom_call_target="tpu_custom_call" | custom-call | flops 150994944 | bytes 4000000 | tf_op jit(solution)/shard_map/pallas_call | solution.py:140
  13.4 0.1 collective-permute-start.3
  13.5 0.7 fusion.6
  14.2 2.1 %collective-permute-done.3 = bf16[16,16,2304]{2,1,0:T(8,128)(2,1)S(1)} collective-permute-done((bf16[16,16,2304]{2,1,0:T(8,128)(2,1)S(1)}, bf16[16,16,2304]{2,1,0:T(8,128)(2,1)S(1)}, u32[]{:S(2)}, u32[]{:S(2)}) %collective-permute-start.3) | collective-permute-done | bytes 1179680 | tf_op jit(solution)/shard_map/ppermute | solution.py:272
  16.4 0.8 fusion.5
  17.1 2.8 %collective-permute-start.14 = (bf16[4,16,2304]{2,1,0:T(8,128)(2,1)S(1)}, bf16[4,16,2304]{2,1,0:T(8,128)(2,1)S(1)}, u32[]{:S(2)}, u32[]{:S(2)}) collective-permute-start(bf16[4,16,2304]{2,1,0:T(8,128)(2,1)S(1)} %pad_maximum_fusion.12.refs_2_), channel_id=1, source_target_pairs={{0,192},{64,0},{128,64},{192,128},{1,193},{65,1},{129,65},{193,129... | collective-permute-start | bytes 884744 | tf_op jit(solution)/shard_map/ppermute | solution.py:241
  20.0 2.0 %collective-permute-start.8 = (bf16[4,16,2304]{2,1,0:T(8,128)(2,1)S(1)}, bf16[4,16,2304]{2,1,0:T(8,128)(2,1)S(1)}, u32[]{:S(2)}, u32[]{:S(2)}) collective-permute-start(bf16[4,16,2304]{2,1,0:T(8,128)(2,1)S(1)} %pad_maximum_fusion.10), channel_id=1, source_target_pairs={{0,8},{4,12},{8,16},{12,20},{16,24},{20,28},{24,32},{28,36},{32,40... | collective-permute-start | bytes 884744 | tf_op jit(solution)/shard_map/ppermute | solution.py:241
  22.0 0.2 collective-permute-start.9
  22.2 4.3 %collective-permute-done.14.refs_1_ = bf16[4,16,2304]{2,1,0:T(8,128)(2,1)S(1)} collective-permute-done((bf16[4,16,2304]{2,1,0:T(8,128)(2,1)S(1)}, bf16[4,16,2304]{2,1,0:T(8,128)(2,1)S(1)}, u32[]{:S(2)}, u32[]{:S(2)}) %collective-permute-start.14) | collective-permute-done | bytes 294944 | tf_op jit(solution)/shard_map/ppermute | solution.py:241
  26.6 3.4 %collective-permute-done.10.refs_0_ = bf16[4,16,2304]{2,1,0:T(8,128)(2,1)S(1)} collective-permute-done((bf16[4,16,2304]{2,1,0:T(8,128)(2,1)S(1)}, bf16[4,16,2304]{2,1,0:T(8,128)(2,1)S(1)}, u32[]{:S(2)}, u32[]{:S(2)}) %collective-permute-start.10) | collective-permute-done | bytes 294944 | tf_op jit(solution)/shard_map/ppermute | solution.py:241
  30.0 0.7 copy-done.19
  30.7 0.1 collective-permute-done.9.refs_6_
  30.8 0.2 pad_maximum_fusion.5
  31.0 0.4 copy-done.11
  31.4 0.1 copy-done.12
  31.5 2.9 %collective-permute-start.15 = (bf16[10,16,2304]{2,1,0:T(8,128)(2,1)S(1)}, bf16[10,16,2304]{2,1,0:T(8,128)(2,1)S(1)}, u32[]{:S(2)}, u32[]{:S(2)}) collective-permute-start(bf16[10,16,2304]{2,1,0:T(8,128)(2,1)S(1)} %get-tuple-element.32), channel_id=1, source_target_pairs={{0,192},{64,0},{128,64},{192,128},{1,193},{65,1},{129,65},{193,129... | collective-permute-start | bytes 2211848 | tf_op jit(solution)/shard_map/ppermute | solution.py:241
  34.5 5.6 %collective-permute-start.6 = (bf16[4,16,2304]{2,1,0:T(8,128)(2,1)S(1)}, bf16[4,16,2304]{2,1,0:T(8,128)(2,1)S(1)}, u32[]{:S(2)}, u32[]{:S(2)}) collective-permute-start(bf16[4,16,2304]{2,1,0:T(8,128)(2,1)S(1)} %pad_maximum_fusion.8), channel_id=1, source_target_pairs={{0,16},{4,20},{8,24},{12,28},{16,32},{20,36},{24,40},{28,44},{32,4... | collective-permute-start | bytes 884744 | tf_op jit(solution)/shard_map/ppermute | solution.py:241
  40.1 0.1 collective-permute-start.7
  40.2 8.7 %collective-permute-done.15.refs_4_ = bf16[10,16,2304]{2,1,0:T(8,128)(2,1)S(1)} collective-permute-done((bf16[10,16,2304]{2,1,0:T(8,128)(2,1)S(1)}, bf16[10,16,2304]{2,1,0:T(8,128)(2,1)S(1)}, u32[]{:S(2)}, u32[]{:S(2)}) %collective-permute-start.15) | collective-permute-done | bytes 737312 | tf_op jit(solution)/shard_map/ppermute | solution.py:241
  48.9 3.4 %collective-permute-done.11.refs_3_ = bf16[10,16,2304]{2,1,0:T(8,128)(2,1)S(1)} collective-permute-done((bf16[10,16,2304]{2,1,0:T(8,128)(2,1)S(1)}, bf16[10,16,2304]{2,1,0:T(8,128)(2,1)S(1)}, u32[]{:S(2)}, u32[]{:S(2)}) %collective-permute-start.11) | collective-permute-done | bytes 737312 | tf_op jit(solution)/shard_map/ppermute | solution.py:241
  52.4 0.9 collective-permute-done.7.refs_10_
  53.2 0.2 pad_maximum_fusion.2
  53.5 0.5 copy-done.14
  53.9 3.0 %collective-permute-start.16 = (bf16[12,16,2304]{2,1,0:T(8,128)(2,1)S(1)}, bf16[12,16,2304]{2,1,0:T(8,128)(2,1)S(1)}, u32[]{:S(2)}, u32[]{:S(2)}) collective-permute-start(bf16[12,16,2304]{2,1,0:T(8,128)(2,1)S(1)} %get-tuple-element.30), channel_id=1, source_target_pairs={{0,192},{64,0},{128,64},{192,128},{1,193},{65,1},{129,65},{193,129... | collective-permute-start | bytes 2654216 | tf_op jit(solution)/shard_map/ppermute | solution.py:241
  57.0 4.0 %collective-permute-start.4 = (bf16[4,16,2304]{2,1,0:T(8,128)(2,1)S(1)}, bf16[4,16,2304]{2,1,0:T(8,128)(2,1)S(1)}, u32[]{:S(2)}, u32[]{:S(2)}) collective-permute-start(bf16[4,16,2304]{2,1,0:T(8,128)(2,1)S(1)} %pad_maximum_fusion.6), channel_id=1, source_target_pairs={{0,24},{4,28},{8,32},{12,36},{16,40},{20,44},{24,48},{28,52},{32,5... | collective-permute-start | bytes 884744 | tf_op jit(solution)/shard_map/ppermute | solution.py:241
  61.0 1.2 collective-permute-start.5
  62.2 10.6 %collective-permute-done.16.refs_8_ = bf16[12,16,2304]{2,1,0:T(8,128)(2,1)S(1)} collective-permute-done((bf16[12,16,2304]{2,1,0:T(8,128)(2,1)S(1)}, bf16[12,16,2304]{2,1,0:T(8,128)(2,1)S(1)}, u32[]{:S(2)}, u32[]{:S(2)}) %collective-permute-start.16) | collective-permute-done | bytes 884768 | tf_op jit(solution)/shard_map/ppermute | solution.py:241
  72.8 3.4 %collective-permute-done.12.refs_7_ = bf16[12,16,2304]{2,1,0:T(8,128)(2,1)S(1)} collective-permute-done((bf16[12,16,2304]{2,1,0:T(8,128)(2,1)S(1)}, bf16[12,16,2304]{2,1,0:T(8,128)(2,1)S(1)}, u32[]{:S(2)}, u32[]{:S(2)}) %collective-permute-start.12) | collective-permute-done | bytes 884768 | tf_op jit(solution)/shard_map/ppermute | solution.py:241
  76.3 0.0 copy-start.24
  76.3 5.3 %collective-permute-done.5.refs_3_ = bf16[4,16,2304]{2,1,0:T(8,128)(2,1)S(1)} collective-permute-done((bf16[4,16,2304]{2,1,0:T(8,128)(2,1)S(1)}, bf16[4,16,2304]{2,1,0:T(8,128)(2,1)S(1)}, u32[]{:S(2)}, u32[]{:S(2)}) %collective-permute-start.5) | collective-permute-done | bytes 294944 | tf_op jit(solution)/shard_map/ppermute | solution.py:241
  81.6 1.1 pad_maximum_fusion.3
  82.7 2.6 %collective-permute-start.17 = (bf16[12,16,2304]{2,1,0:T(8,128)(2,1)}, bf16[12,16,2304]{2,1,0:T(8,128)(2,1)S(1)}, u32[]{:S(2)}, u32[]{:S(2)}) collective-permute-start(bf16[12,16,2304]{2,1,0:T(8,128)(2,1)} %get-tuple-element.28), channel_id=1, source_target_pairs={{0,192},{64,0},{128,64},{192,128},{1,193},{65,1},{129,65},{193,129... | collective-permute-start | bytes 2654216 | tf_op jit(solution)/shard_map/ppermute | solution.py:241
  85.3 0.1 stack.67
  85.4 0.7 convert_reduce_fusion
  86.1 1.8 %collective-permute-start.18 = (bf16[4,16,2304]{2,1,0:T(8,128)(2,1)S(1)}, bf16[4,16,2304]{2,1,0:T(8,128)(2,1)S(1)}, u32[]{:S(2)}, u32[]{:S(2)}) collective-permute-start(bf16[4,16,2304]{2,1,0:T(8,128)(2,1)S(1)} %pad_maximum_fusion.13), channel_id=1, source_target_pairs={{0,32},{4,36},{8,40},{12,44},{16,48},{20,52},{24,56},{28,60},{32,0... | collective-permute-start | bytes 884744 | tf_op jit(solution)/shard_map/ppermute | solution.py:241
  87.9 0.1 select_reduce_fusion.1
  88.0 0.1 iota_compare_fusion.1
  88.1 13.0 %collective-permute-done.18.refs_8_ = bf16[4,16,2304]{2,1,0:T(8,128)(2,1)S(1)} collective-permute-done((bf16[4,16,2304]{2,1,0:T(8,128)(2,1)S(1)}, bf16[4,16,2304]{2,1,0:T(8,128)(2,1)S(1)}, u32[]{:S(2)}, u32[]{:S(2)}) %collective-permute-start.18) | collective-permute-done | bytes 294944 | tf_op jit(solution)/shard_map/ppermute | solution.py:241
  101.0 1.5 %collective-permute-start.23 = (bf16[4,16,2304]{2,1,0:T(8,128)(2,1)S(1)}, bf16[4,16,2304]{2,1,0:T(8,128)(2,1)}, u32[]{:S(2)}, u32[]{:S(2)}) collective-permute-start(bf16[4,16,2304]{2,1,0:T(8,128)(2,1)S(1)} %collective-permute-done.18.refs_8_), channel_id=1, source_target_pairs={{0,128},{64,192},{128,0},{192,64},{1,129},{65,193},{129,1},{193,65... | collective-permute-start | bytes 884744 | tf_op jit(solution)/shard_map/ppermute | solution.py:241
  102.6 1.5 %collective-permute-start.21 = (bf16[4,16,2304]{2,1,0:T(8,128)(2,1)S(1)}, bf16[4,16,2304]{2,1,0:T(8,128)(2,1)}, u32[]{:S(2)}, u32[]{:S(2)}) collective-permute-start(bf16[4,16,2304]{2,1,0:T(8,128)(2,1)S(1)} %collective-permute-done.18.refs_8_), channel_id=1, source_target_pairs={{0,192},{64,0},{128,64},{192,128},{1,193},{65,1},{129,65},{193,129... | collective-permute-start | bytes 884744 | tf_op jit(solution)/shard_map/ppermute | solution.py:241
  104.1 0.9 collective-permute-start.19
  105.0 2.6 %collective-permute-start.22 = (bf16[4,16,2304]{2,1,0:T(8,128)(2,1)S(1)}, bf16[4,16,2304]{2,1,0:T(8,128)(2,1)}, u32[]{:S(2)}, u32[]{:S(2)}) collective-permute-start(bf16[4,16,2304]{2,1,0:T(8,128)(2,1)S(1)} %slice.107), channel_id=1, source_target_pairs={{0,192},{64,0},{128,64},{192,128},{1,193},{65,1},{129,65},{193,129... | collective-permute-start | bytes 884744 | tf_op jit(solution)/shard_map/ppermute | solution.py:241
  107.7 7.0 %collective-permute-done.13.refs_0_ = bf16[12,16,2304]{2,1,0:T(8,128)(2,1)S(1)} collective-permute-done((bf16[12,16,2304]{2,1,0:T(8,128)(2,1)S(1)}, bf16[12,16,2304]{2,1,0:T(8,128)(2,1)S(1)}, u32[]{:S(2)}, u32[]{:S(2)}) %collective-permute-start.13) | collective-permute-done | bytes 884768 | tf_op jit(solution)/shard_map/ppermute | solution.py:241
  114.6 0.1 collective-permute-start.20
  114.7 0.1 select_reduce_fusion
  114.9 0.1 copy.8
  114.9 0.6 reshape.68.dest_ref
  115.6 8.2 %shard_map.66.refs_10_ = bf16[32,4,1,16,2304]{4,3,2,1,0:T(8,128)(2,1)} custom-call(s32[32]{0:T(128)} %reshape.68.dest_ref, s32[1]{0:T(128)} %bitcast.16.count_ref, s32[1]{0:T(128)} %bitcast.17.relay_ref, bf16[4,16,2304]{2,1,0:T(8,128)(2,1)} %copy-done.19, bf16[4,16,2304]{2,1,0:T(8,128)(2,1)} %copy-done.18, bf16[4,16,2304]{2,1,0:T(8,128)(2,1)} %copy-done.17, ...), custom_call_target="tpu_custom_call" | custom-call | bytes 10616832 | tf_op jit(solution)/shard_map/pallas_call | solution.py:226
  123.8 0.7 collective-permute-done.22.refs_7_
  124.5 1.5 %collective-permute-done.20.refs_5_ = bf16[4,16,2304]{2,1,0:T(8,128)(2,1)S(1)} collective-permute-done((bf16[4,16,2304]{2,1,0:T(8,128)(2,1)S(1)}, bf16[4,16,2304]{2,1,0:T(8,128)(2,1)S(1)}, u32[]{:S(2)}, u32[]{:S(2)}) %collective-permute-start.20) | collective-permute-done | bytes 294944 | tf_op jit(solution)/shard_map/ppermute | solution.py:241
  126.0 0.7 copy-done.23
  126.7 4.5 %shard_map.67 = bf16[32,4,1,16,2304]{4,3,2,1,0:T(8,128)(2,1)} custom-call(s32[32]{0:T(128)} %reshape.68.dest_ref, s32[1]{0:T(128)} %bitcast.16.count_ref, s32[1]{0:T(128)} %bitcast.17.relay_ref, bf16[12,16,2304]{2,1,0:T(8,128)(2,1)} %copy-done.8, bf16[12,16,2304]{2,1,0:T(8,128)(2,1)} %copy-done.7, ...), custom_call_target="tpu_custom_call", output_to_operand_aliasing={{}: (13, {})} | custom-call | bytes 8257536 | tf_op jit(solution)/shard_map/pallas_call | solution.py:226
  (70 shorter events, 0.5 us)
Async XLA Ops:
  0.0 10.0 %collective-permute-start.2 = (bf16[3,64,192]{2,1,0:T(8,128)(2,1)}, bf16[3,64,192]{2,1,0:T(8,128)(2,1)S(1)}, u32[]{:S(2)}, u32[]{:S(2)}) collective-permute-start(bf16[3,64,192]{2,1,0:T(8,128)(2,1)} %bitcast.34), channel_id=1, source_target_pairs={{0,3},{1,0},{2,1},{3,2},{4,7},{5,4},{6,5},{7,6},{8,11},{9,8},{10,9... | collective-permute-start | bytes 221192 | tf_op jit(solution)/shard_map/ppermute | solution.py:241
  3.0 7.1 %collective-permute-start.1 = (bf16[3,64,192]{2,1,0:T(8,128)(2,1)}, bf16[3,64,192]{2,1,0:T(8,128)(2,1)S(1)}, u32[]{:S(2)}, u32[]{:S(2)}) collective-permute-start(bf16[3,64,192]{2,1,0:T(8,128)(2,1)} %bitcast.35), channel_id=1, source_target_pairs={{0,2},{1,3},{2,0},{3,1},{4,6},{5,7},{6,4},{7,5},{8,10},{9,11},{10,... | collective-permute-start | bytes 221192 | tf_op jit(solution)/shard_map/ppermute | solution.py:241
  3.6 7.4 %collective-permute-start = (bf16[3,64,192]{2,1,0:T(8,128)(2,1)}, bf16[3,64,192]{2,1,0:T(8,128)(2,1)S(1)}, u32[]{:S(2)}, u32[]{:S(2)}) collective-permute-start(bf16[3,64,192]{2,1,0:T(8,128)(2,1)} %bitcast.36), channel_id=1, source_target_pairs={{0,1},{1,2},{2,3},{3,0},{4,5},{5,6},{6,7},{7,4},{8,9},{9,10},{10,1... | collective-permute-start | bytes 221192 | tf_op jit(solution)/shard_map/ppermute | solution.py:241
  6.2 1.0 copy-start
  7.2 1.0 copy-start.1
  8.2 1.0 copy-start.2
  9.2 1.9 %copy-start.3 = (bf16[1,3,256,64]{2,3,1,0:T(8,128)(2,1)S(1)}, bf16[1,3,256,64]{2,3,1,0:T(8,128)(2,1)}, u32[]{:S(2)}) copy-start(bf16[1,3,256,64]{2,3,1,0:T(8,128)(2,1)} %param.9) | copy-start | bytes 294916
  9.2 1.9 %copy-start.4 = (bf16[1,3,64,192]{3,2,1,0:T(8,128)(2,1)S(1)}, bf16[1,3,64,192]{3,2,1,0:T(8,128)(2,1)}, u32[]{:S(2)}) copy-start(bf16[1,3,64,192]{3,2,1,0:T(8,128)(2,1)} %param.10) | copy-start | bytes 221188
  13.4 2.9 %collective-permute-start.3 = (bf16[16,16,2304]{2,1,0:T(8,128)(2,1)S(1)}, bf16[16,16,2304]{2,1,0:T(8,128)(2,1)S(1)}, u32[]{:S(2)}, u32[]{:S(2)}) collective-permute-start(bf16[16,16,2304]{2,1,0:T(8,128)(2,1)S(1)} %get-tuple-element.9), channel_id=1, source_target_pairs={{0,4},{4,0},{8,12},{12,8},{16,20},{20,16},{24,28},{28,24},{32,36},... | collective-permute-start | bytes 3538952 | tf_op jit(solution)/shard_map/ppermute | solution.py:272
  17.1 12.9 %copy-start.17 = (bf16[4,16,2304]{2,1,0:T(8,128)(2,1)}, bf16[4,16,2304]{2,1,0:T(8,128)(2,1)S(1)}, u32[]{:S(2)}) copy-start(bf16[4,16,2304]{2,1,0:T(8,128)(2,1)S(1)} %pad_maximum_fusion.12.refs_2_) | copy-start | bytes 884740
  17.1 9.4 %collective-permute-start.14 = (bf16[4,16,2304]{2,1,0:T(8,128)(2,1)S(1)}, bf16[4,16,2304]{2,1,0:T(8,128)(2,1)S(1)}, u32[]{:S(2)}, u32[]{:S(2)}) collective-permute-start(bf16[4,16,2304]{2,1,0:T(8,128)(2,1)S(1)} %pad_maximum_fusion.12.refs_2_), channel_id=1, source_target_pairs={{0,192},{64,0},{128,64},{192,128},{1,193},{65,1},{129,65},{193,129... | collective-permute-start | bytes 884744 | tf_op jit(solution)/shard_map/ppermute | solution.py:241
  20.0 10.0 %collective-permute-start.10 = (bf16[4,16,2304]{2,1,0:T(8,128)(2,1)S(1)}, bf16[4,16,2304]{2,1,0:T(8,128)(2,1)S(1)}, u32[]{:S(2)}, u32[]{:S(2)}) collective-permute-start(bf16[4,16,2304]{2,1,0:T(8,128)(2,1)S(1)} %pad_maximum_fusion.12.refs_2_), channel_id=1, source_target_pairs={{0,64},{64,128},{128,192},{192,0},{1,65},{65,129},{129,193},{193,1... | collective-permute-start | bytes 884744 | tf_op jit(solution)/shard_map/ppermute | solution.py:241
  20.0 10.0 %collective-permute-start.8 = (bf16[4,16,2304]{2,1,0:T(8,128)(2,1)S(1)}, bf16[4,16,2304]{2,1,0:T(8,128)(2,1)S(1)}, u32[]{:S(2)}, u32[]{:S(2)}) collective-permute-start(bf16[4,16,2304]{2,1,0:T(8,128)(2,1)S(1)} %pad_maximum_fusion.10), channel_id=1, source_target_pairs={{0,8},{4,12},{8,16},{12,20},{16,24},{20,28},{24,32},{28,36},{32,40... | collective-permute-start | bytes 884744 | tf_op jit(solution)/shard_map/ppermute | solution.py:241
  22.0 8.7 %collective-permute-start.9 = (bf16[4,16,2304]{2,1,0:T(8,128)(2,1)S(1)}, bf16[4,16,2304]{2,1,0:T(8,128)(2,1)S(1)}, u32[]{:S(2)}, u32[]{:S(2)}) collective-permute-start(bf16[4,16,2304]{2,1,0:T(8,128)(2,1)S(1)} %pad_maximum_fusion.11), channel_id=1, source_target_pairs={{0,56},{4,60},{8,0},{12,4},{16,8},{20,12},{24,16},{28,20},{32,24},... | collective-permute-start | bytes 884744 | tf_op jit(solution)/shard_map/ppermute | solution.py:241
  26.6 3.5 %copy-start.18 = (bf16[4,16,2304]{2,1,0:T(8,128)(2,1)}, bf16[4,16,2304]{2,1,0:T(8,128)(2,1)S(1)}, u32[]{:S(2)}) copy-start(bf16[4,16,2304]{2,1,0:T(8,128)(2,1)S(1)} %collective-permute-done.14.refs_1_) | copy-start | bytes 884740
  30.0 0.7 copy-start.19
  30.7 0.7 copy-start.11
  30.8 0.7 copy-start.12
  31.5 17.4 %collective-permute-start.15 = (bf16[10,16,2304]{2,1,0:T(8,128)(2,1)S(1)}, bf16[10,16,2304]{2,1,0:T(8,128)(2,1)S(1)}, u32[]{:S(2)}, u32[]{:S(2)}) collective-permute-start(bf16[10,16,2304]{2,1,0:T(8,128)(2,1)S(1)} %get-tuple-element.32), channel_id=1, source_target_pairs={{0,192},{64,0},{128,64},{192,128},{1,193},{65,1},{129,65},{193,129... | collective-permute-start | bytes 2211848 | tf_op jit(solution)/shard_map/ppermute | solution.py:241
  34.4 17.9 %collective-permute-start.11 = (bf16[10,16,2304]{2,1,0:T(8,128)(2,1)S(1)}, bf16[10,16,2304]{2,1,0:T(8,128)(2,1)S(1)}, u32[]{:S(2)}, u32[]{:S(2)}) collective-permute-start(bf16[10,16,2304]{2,1,0:T(8,128)(2,1)S(1)} %get-tuple-element.33), channel_id=1, source_target_pairs={{0,64},{64,128},{128,192},{192,0},{1,65},{65,129},{129,193},{193,1... | collective-permute-start | bytes 2211848 | tf_op jit(solution)/shard_map/ppermute | solution.py:241
  34.5 17.9 %collective-permute-start.6 = (bf16[4,16,2304]{2,1,0:T(8,128)(2,1)S(1)}, bf16[4,16,2304]{2,1,0:T(8,128)(2,1)S(1)}, u32[]{:S(2)}, u32[]{:S(2)}) collective-permute-start(bf16[4,16,2304]{2,1,0:T(8,128)(2,1)S(1)} %pad_maximum_fusion.8), channel_id=1, source_target_pairs={{0,16},{4,20},{8,24},{12,28},{16,32},{20,36},{24,40},{28,44},{32,4... | collective-permute-start | bytes 884744 | tf_op jit(solution)/shard_map/ppermute | solution.py:241
  40.1 13.1 %collective-permute-start.7 = (bf16[4,16,2304]{2,1,0:T(8,128)(2,1)S(1)}, bf16[4,16,2304]{2,1,0:T(8,128)(2,1)S(1)}, u32[]{:S(2)}, u32[]{:S(2)}) collective-permute-start(bf16[4,16,2304]{2,1,0:T(8,128)(2,1)S(1)} %pad_maximum_fusion.9), channel_id=1, source_target_pairs={{0,48},{4,52},{8,56},{12,60},{16,0},{20,4},{24,8},{28,12},{32,16},... | collective-permute-start | bytes 884744 | tf_op jit(solution)/shard_map/ppermute | solution.py:241
  48.9 4.5 %copy-start.9 = (bf16[10,16,2304]{2,1,0:T(8,128)(2,1)}, bf16[10,16,2304]{2,1,0:T(8,128)(2,1)S(1)}, u32[]{:S(2)}) copy-start(bf16[10,16,2304]{2,1,0:T(8,128)(2,1)S(1)} %collective-permute-done.15.refs_4_) | copy-start | bytes 2211844
  52.3 1.1 copy-start.10
  52.3 1.1 copy-start.13
  53.2 0.7 copy-start.14
  53.9 18.9 %collective-permute-start.16 = (bf16[12,16,2304]{2,1,0:T(8,128)(2,1)S(1)}, bf16[12,16,2304]{2,1,0:T(8,128)(2,1)S(1)}, u32[]{:S(2)}, u32[]{:S(2)}) collective-permute-start(bf16[12,16,2304]{2,1,0:T(8,128)(2,1)S(1)} %get-tuple-element.30), channel_id=1, source_target_pairs={{0,192},{64,0},{128,64},{192,128},{1,193},{65,1},{129,65},{193,129... | collective-permute-start | bytes 2654216 | tf_op jit(solution)/shard_map/ppermute | solution.py:241
  56.9 19.3 %collective-permute-start.12 = (bf16[12,16,2304]{2,1,0:T(8,128)(2,1)S(1)}, bf16[12,16,2304]{2,1,0:T(8,128)(2,1)S(1)}, u32[]{:S(2)}, u32[]{:S(2)}) collective-permute-start(bf16[12,16,2304]{2,1,0:T(8,128)(2,1)S(1)} %get-tuple-element.31), channel_id=1, source_target_pairs={{0,64},{64,128},{128,192},{192,0},{1,65},{65,129},{129,193},{193,1... | collective-permute-start | bytes 2654216 | tf_op jit(solution)/shard_map/ppermute | solution.py:241
  57.0 19.3 %collective-permute-start.4 = (bf16[4,16,2304]{2,1,0:T(8,128)(2,1)S(1)}, bf16[4,16,2304]{2,1,0:T(8,128)(2,1)S(1)}, u32[]{:S(2)}, u32[]{:S(2)}) collective-permute-start(bf16[4,16,2304]{2,1,0:T(8,128)(2,1)S(1)} %pad_maximum_fusion.6), channel_id=1, source_target_pairs={{0,24},{4,28},{8,32},{12,36},{16,40},{20,44},{24,48},{28,52},{32,5... | collective-permute-start | bytes 884744 | tf_op jit(solution)/shard_map/ppermute | solution.py:241
  61.0 20.6 %collective-permute-start.5 = (bf16[4,16,2304]{2,1,0:T(8,128)(2,1)S(1)}, bf16[4,16,2304]{2,1,0:T(8,128)(2,1)S(1)}, u32[]{:S(2)}, u32[]{:S(2)}) collective-permute-start(bf16[4,16,2304]{2,1,0:T(8,128)(2,1)S(1)} %pad_maximum_fusion.7), channel_id=1, source_target_pairs={{0,40},{4,44},{8,48},{12,52},{16,56},{20,60},{24,0},{28,4},{32,8},... | collective-permute-start | bytes 884744 | tf_op jit(solution)/shard_map/ppermute | solution.py:241
  72.8 9.9 %copy-start.5 = (bf16[12,16,2304]{2,1,0:T(8,128)(2,1)}, bf16[12,16,2304]{2,1,0:T(8,128)(2,1)S(1)}, u32[]{:S(2)}) copy-start(bf16[12,16,2304]{2,1,0:T(8,128)(2,1)S(1)} %collective-permute-done.16.refs_8_) | copy-start | bytes 2654212
  76.2 6.5 %copy-start.6 = (bf16[12,16,2304]{2,1,0:T(8,128)(2,1)}, bf16[12,16,2304]{2,1,0:T(8,128)(2,1)S(1)}, u32[]{:S(2)}) copy-start(bf16[12,16,2304]{2,1,0:T(8,128)(2,1)S(1)} %collective-permute-done.12.refs_7_) | copy-start | bytes 2654212
  76.3 9.1 %copy-start.24 = (s32[16,16]{1,0:T(8,128)S(1)}, s32[16,16]{1,0:T(8,128)}, u32[]{:S(2)}) copy-start(s32[16,16]{1,0:T(8,128)} %param.11) | copy-start | bytes 3076
  76.3 9.8 %copy-start.20 = (bf16[2,16,2304]{2,1,0:T(8,128)(2,1)S(1)}, bf16[2,16,2304]{2,1,0:T(8,128)(2,1)}, u32[]{:S(2)}) copy-start(bf16[2,16,2304]{2,1,0:T(8,128)(2,1)} %get-tuple-element.21) | copy-start | bytes 442372
  76.3 9.8 %copy-start.21 = (bf16[2,16,2304]{2,1,0:T(8,128)(2,1)S(1)}, bf16[2,16,2304]{2,1,0:T(8,128)(2,1)}, u32[]{:S(2)}) copy-start(bf16[2,16,2304]{2,1,0:T(8,128)(2,1)} %get-tuple-element.13) | copy-start | bytes 442372
  76.3 6.4 %copy-start.15 = (bf16[4,16,2304]{2,1,0:T(8,128)(2,1)}, bf16[4,16,2304]{2,1,0:T(8,128)(2,1)S(1)}, u32[]{:S(2)}) copy-start(bf16[4,16,2304]{2,1,0:T(8,128)(2,1)S(1)} %collective-permute-done.4.refs_2_) | copy-start | bytes 884740
  81.6 1.1 copy-start.16
  82.7 22.3 %collective-permute-start.17 = (bf16[12,16,2304]{2,1,0:T(8,128)(2,1)}, bf16[12,16,2304]{2,1,0:T(8,128)(2,1)S(1)}, u32[]{:S(2)}, u32[]{:S(2)}) collective-permute-start(bf16[12,16,2304]{2,1,0:T(8,128)(2,1)} %get-tuple-element.28), channel_id=1, source_target_pairs={{0,192},{64,0},{128,64},{192,128},{1,193},{65,1},{129,65},{193,129... | collective-permute-start | bytes 2654216 | tf_op jit(solution)/shard_map/ppermute | solution.py:241
  85.3 29.3 %collective-permute-start.13 = (bf16[12,16,2304]{2,1,0:T(8,128)(2,1)S(1)}, bf16[12,16,2304]{2,1,0:T(8,128)(2,1)S(1)}, u32[]{:S(2)}, u32[]{:S(2)}) collective-permute-start(bf16[12,16,2304]{2,1,0:T(8,128)(2,1)S(1)} %get-tuple-element.29), channel_id=1, source_target_pairs={{0,64},{64,128},{128,192},{192,0},{1,65},{65,129},{129,193},{193,1... | collective-permute-start | bytes 2654216 | tf_op jit(solution)/shard_map/ppermute | solution.py:241
  86.1 15.0 %collective-permute-start.18 = (bf16[4,16,2304]{2,1,0:T(8,128)(2,1)S(1)}, bf16[4,16,2304]{2,1,0:T(8,128)(2,1)S(1)}, u32[]{:S(2)}, u32[]{:S(2)}) collective-permute-start(bf16[4,16,2304]{2,1,0:T(8,128)(2,1)S(1)} %pad_maximum_fusion.13), channel_id=1, source_target_pairs={{0,32},{4,36},{8,40},{12,44},{16,48},{20,52},{24,56},{28,60},{32,0... | collective-permute-start | bytes 884744 | tf_op jit(solution)/shard_map/ppermute | solution.py:241
  101.0 22.7 %copy-start.22 = (bf16[4,16,2304]{2,1,0:T(8,128)(2,1)}, bf16[4,16,2304]{2,1,0:T(8,128)(2,1)S(1)}, u32[]{:S(2)}) copy-start(bf16[4,16,2304]{2,1,0:T(8,128)(2,1)S(1)} %collective-permute-done.18.refs_8_) | copy-start | bytes 884740
  101.0 22.8 %collective-permute-start.23 = (bf16[4,16,2304]{2,1,0:T(8,128)(2,1)S(1)}, bf16[4,16,2304]{2,1,0:T(8,128)(2,1)}, u32[]{:S(2)}, u32[]{:S(2)}) collective-permute-start(bf16[4,16,2304]{2,1,0:T(8,128)(2,1)S(1)} %collective-permute-done.18.refs_8_), channel_id=1, source_target_pairs={{0,128},{64,192},{128,0},{192,64},{1,129},{65,193},{129,1},{193,65... | collective-permute-start | bytes 884744 | tf_op jit(solution)/shard_map/ppermute | solution.py:241
  102.6 21.2 %collective-permute-start.21 = (bf16[4,16,2304]{2,1,0:T(8,128)(2,1)S(1)}, bf16[4,16,2304]{2,1,0:T(8,128)(2,1)}, u32[]{:S(2)}, u32[]{:S(2)}) collective-permute-start(bf16[4,16,2304]{2,1,0:T(8,128)(2,1)S(1)} %collective-permute-done.18.refs_8_), channel_id=1, source_target_pairs={{0,192},{64,0},{128,64},{192,128},{1,193},{65,1},{129,65},{193,129... | collective-permute-start | bytes 884744 | tf_op jit(solution)/shard_map/ppermute | solution.py:241
  104.1 19.7 %collective-permute-start.19 = (bf16[4,16,2304]{2,1,0:T(8,128)(2,1)S(1)}, bf16[4,16,2304]{2,1,0:T(8,128)(2,1)}, u32[]{:S(2)}, u32[]{:S(2)}) collective-permute-start(bf16[4,16,2304]{2,1,0:T(8,128)(2,1)S(1)} %collective-permute-done.18.refs_8_), channel_id=1, source_target_pairs={{0,64},{64,128},{128,192},{192,0},{1,65},{65,129},{129,193},{193,1... | collective-permute-start | bytes 884744 | tf_op jit(solution)/shard_map/ppermute | solution.py:241
  105.0 18.8 %copy-start.7 = (bf16[12,16,2304]{2,1,0:T(8,128)(2,1)}, bf16[12,16,2304]{2,1,0:T(8,128)(2,1)S(1)}, u32[]{:S(2)}) copy-start(bf16[12,16,2304]{2,1,0:T(8,128)(2,1)S(1)} %collective-permute-done.17.refs_1_) | copy-start | bytes 2654212
  105.0 19.5 %collective-permute-start.22 = (bf16[4,16,2304]{2,1,0:T(8,128)(2,1)S(1)}, bf16[4,16,2304]{2,1,0:T(8,128)(2,1)}, u32[]{:S(2)}, u32[]{:S(2)}) collective-permute-start(bf16[4,16,2304]{2,1,0:T(8,128)(2,1)S(1)} %slice.107), channel_id=1, source_target_pairs={{0,192},{64,0},{128,64},{192,128},{1,193},{65,1},{129,65},{193,129... | collective-permute-start | bytes 884744 | tf_op jit(solution)/shard_map/ppermute | solution.py:241
  114.6 9.2 %copy-start.8 = (bf16[12,16,2304]{2,1,0:T(8,128)(2,1)}, bf16[12,16,2304]{2,1,0:T(8,128)(2,1)S(1)}, u32[]{:S(2)}) copy-start(bf16[12,16,2304]{2,1,0:T(8,128)(2,1)S(1)} %collective-permute-done.13.refs_0_) | copy-start | bytes 2654212
  114.6 11.4 %collective-permute-start.20 = (bf16[4,16,2304]{2,1,0:T(8,128)(2,1)S(1)}, bf16[4,16,2304]{2,1,0:T(8,128)(2,1)S(1)}, u32[]{:S(2)}, u32[]{:S(2)}) collective-permute-start(bf16[4,16,2304]{2,1,0:T(8,128)(2,1)S(1)} %slice.106), channel_id=1, source_target_pairs={{0,64},{64,128},{128,192},{192,0},{1,65},{65,129},{129,193},{193,1... | collective-permute-start | bytes 884744 | tf_op jit(solution)/shard_map/ppermute | solution.py:241
  126.0 0.7 copy-start.23

commit v2 on v1

--- a/solution.py
+++ b/solution.py
@@ -281,11 +281,11 @@
 
     near = jnp.concatenate([own, got[:PAIR]], axis=0)
     steps = [
-        ([0], [near], False, False),
-        ([1, chips - 1], None, False, False),
-        ([2, chips - 2], None, False, True),
-        ([3, chips - 3], None, False, False),
-        ([4], None, True, True),
+        ([0], [near], False, False, 2),
+        ([1, chips - 1], None, False, False, 1),
+        ([2, chips - 2], None, False, True, 1),
+        ([3, chips - 3], None, False, False, 1),
+        ([4], None, True, True, 0),
     ]
     sources = jnp.stack(
         [((me - 2 * d) % owners) ^ core for names, *_ in steps for d in names for core in (0, 1)]
@@ -310,11 +310,13 @@
             return [front] + ([rest] if rest else [])
         return [front + rest]
 
-    out, bufs, pieces = None, [], []
-    forward_right, forward_left, entry, earlier = [], [], 0, []
-    for names, items, split, flush in steps:
+    out, bufs, pieces, entry = None, [], [], 0
+    waiting = [[] for _ in range(len(steps) + 2)]
+    for number, (names, items, split, flush, delay) in enumerate(steps):
         items = [send(d) for d in names] if items is None else items
         first, last = items[:1], items[1:]
+        held = waiting[number]
+        forward_right, forward_left = [h[0] for h in held], [h[1] for h in held]
         from_left = ring(messages(first, last, forward_right, split), 1)
         from_right = ring(
             messages(last, first, forward_left, split)
@@ -322,38 +324,42 @@
             else messages(first, last, forward_left, split),
             -1,
         )
-        held = []
+        count = sum(item.shape[0] for item in items)
+        row = count
+        for _, _, entries in held:
+            half = len(entries) // 2
+            for j in range(half):
+                pieces.append((*from_left[row + j], entries[j], 2))
+                pieces.append((*from_right[row + j], entries[half + j], 2))
+            row += half
+        order = []
         for item in items:
             bufs.append(item)
-            held.append([(len(bufs) - 1, row) for row in range(item.shape[0])])
-        count = sum(len(rows) for rows in held)
-        order = held[0] + (held[1] if len(held) == 2 else []) if held else []
-        turned = held[1] + held[0] if len(held) == 2 else order
-        half = len(earlier) // 2
-        pieces += [(*from_left[count + j], earlier[j], 2) for j in range(half)]
-        pieces += [(*from_right[count + j], earlier[half + j], 2) for j in range(half)]
-        base = entry
-        where = {slot: base + j for j, slot in enumerate(order)}
+            order += [(len(bufs) - 1, j) for j in range(item.shape[0])]
+        half = count // 2
+        turned = order[half:] + order[:half] if len(items) == 2 else order
+        where = {slot: entry + j for j, slot in enumerate(order)}
         for j in range(count):
             pieces += [
-                (*order[j], base + j, 0),
+                (*order[j], entry + j, 0),
                 (*from_left[j], where[order[j]], 3),
                 (*from_right[j], where[turned[j]], 1),
             ]
-        earlier = [base + j for j in range(count)]
-        if names == [4]:
+        entries = list(range(entry, entry + count))
+        entry += count
+        if count and delay:
+            left_buf, right_buf = bufs[from_left[0][0]], bufs[from_right[0][0]]
+            start = 0 if len(items) == 2 else half
+            waiting[number + delay].append(
+                (
+                    left_buf if left_buf.shape[0] == half else left_buf[:half],
+                    right_buf if right_buf.shape[0] == half else right_buf[start : start + half],
+                    entries,
+                )
+            )
+        elif count:
             across = ring([items], 2)
-            pieces += [(*across[j], base + j, 2) for j in range(count)]
-        entry += count
-        half = count // 2
-        forward_right = forward_left = []
-        if count:
-            left_buf, right_buf = bufs[from_left[0][0]], bufs[from_right[0][0]]
-            forward_right = [left_buf if left_buf.shape[0] == half else left_buf[:half]]
-            if len(items) == 2:
-                forward_left = [right_buf if right_buf.shape[0] == half else right_buf[:half]]
-            else:
-                forward_left = [right_buf[half:count]]
+            pieces += [(*across[j], entries[j], 2) for j in range(count)]
         if flush:
             out = place(out, pieces, dest, total[None], relay, bufs, out_shape)
             bufs, pieces = [], []

time: 132 us -> 121 us (0.917)
  the two profiles are of different devices: /device:TPU:32 before, /device:TPU:6 now
where the time goes in v2:
time: 121 us; the launch traced here: 120 us
  starting transfers between devices  47.4 us (39%)
  waiting for transfers between devices  46.7 us (39%)
  Pallas kernels  14.8 us (12%)
  local copies, waits for them, and re-layouts  6.74 us (6%)
  other arithmetic  3.54 us (3%)
    ppermute x23, starting transfers between devices, shift(): lax.ppermute(value, axis, [(i, (i + by) % size) for i in range(size)])  47.3 us
    ppermute x23, waiting for transfers between devices, shift(): lax.ppermute(value, axis, [(i, (i + by) % size) for i in range(size)])  44 us
    pallas_call x2, Pallas kernels, place(): pl.pallas_call(functools.partial(place_kernel, pieces, count, first), out...  11.7 us
    unnamed x48, local copies, waits for them, and re-layouts  4.9 us
    ppermute x1, waiting for transfers between devices, body(): got = lax.ppermute(swap, 'expert', mate)  2.75 us
  transfers between devices with their start and end apart: 24, of which 10 were waited for; matrix products, arithmetic and copies ran while one was open for 3% of the time, Pallas kernels for 6%

profile of v2, /device:TPU:6, one launch (start us, length us, event | category | flops | bytes accessed | tf_op | source)
XLA Modules:
  0.0 119.8 jit_solution(1073382021486253584)
XLA Ops:
  0.0 3.0 %collective-permute-start.2 = (bf16[3,64,192]{2,1,0:T(8,128)(2,1)}, bf16[3,64,192]{2,1,0:T(8,128)(2,1)S(1)}, u32[]{:S(2)}, u32[]{:S(2)}) collective-permute-start(bf16[3,64,192]{2,1,0:T(8,128)(2,1)} %bitcast.34), channel_id=1, source_target_pairs={{0,3},{1,0},{2,1},{3,2},{4,7},{5,4},{6,5},{7,6},{8,11},{9,8},{10,9... | collective-permute-start | bytes 221192 | tf_op jit(solution)/shard_map/ppermute | solution.py:241
  3.0 0.6 collective-permute-start.1
  3.6 1.0 collective-permute-start
  4.6 0.7 dynamic-slice_bitcast_fusion
  5.3 0.2 convert_reduce_fusion.2
  5.5 0.7 fusion.3.index_ref
  6.2 1.0 copy-done
  7.2 1.0 copy-done.1
  8.2 1.0 copy-done.2
  9.2 0.8 shard_map.64.woven_ref
  10.0 0.0 collective-permute-done.2.v3
  10.0 0.0 collective-permute-done.1.v2
  10.1 1.0 collective-permute-done.v1
  11.1 2.3 %shard_map.65 = (bf16[2,16,2304]{2,1,0:T(8,128)(2,1)S(1)}, bf16[14,16,2304]{2,1,0:T(8,128)(2,1)S(1)}, bf16[16,16,2304]{2,1,0:T(8,128)(2,1)S(1)}) custom-call(s32[16]{0:T(128)S(1)} %fusion.3.index_ref, s32[1]{0:T(128)} %bitcast.19.tensor_ref, bf16[256,2304]{1,0:T(8,128)(2,1)S(1)} %shard_map.64.woven_ref, bf16[3,64,256]{2,1,0:T(8,128)(2,1)S(1)} %bitcast.33, ...), custom_call_target="tpu_custom_call" | custom-call | flops 150994944 | bytes 4000000 | tf_op jit(solution)/shard_map/pallas_call | solution.py:140
  13.4 0.1 collective-permute-start.3
  13.5 0.1 fusion.6
  13.6 2.8 %collective-permute-done.3 = bf16[16,16,2304]{2,1,0:T(8,128)(2,1)S(1)} collective-permute-done((bf16[16,16,2304]{2,1,0:T(8,128)(2,1)S(1)}, bf16[16,16,2304]{2,1,0:T(8,128)(2,1)S(1)}, u32[]{:S(2)}, u32[]{:S(2)}) %collective-permute-start.3) | collective-permute-done | bytes 1179680 | tf_op jit(solution)/shard_map/ppermute | solution.py:272
  16.4 0.1 fusion.5
  16.5 0.9 collective-permute-start.14
  17.4 2.4 %collective-permute-start.8 = (bf16[4,16,2304]{2,1,0:T(8,128)(2,1)S(1)}, bf16[4,16,2304]{2,1,0:T(8,128)(2,1)S(1)}, u32[]{:S(2)}, u32[]{:S(2)}) collective-permute-start(bf16[4,16,2304]{2,1,0:T(8,128)(2,1)S(1)} %pad_maximum_fusion.10.refs_2_), channel_id=1, source_target_pairs={{0,64},{64,128},{128,192},{192,0},{1,65},{65,129},{129,193},{193,1... | collective-permute-start | bytes 884744 | tf_op jit(solution)/shard_map/ppermute | solution.py:241
  19.8 2.0 %collective-permute-start.9 = (bf16[4,16,2304]{2,1,0:T(8,128)(2,1)S(1)}, bf16[4,16,2304]{2,1,0:T(8,128)(2,1)S(1)}, u32[]{:S(2)}, u32[]{:S(2)}) collective-permute-start(bf16[4,16,2304]{2,1,0:T(8,128)(2,1)S(1)} %pad_maximum_fusion.11), channel_id=1, source_target_pairs={{0,8},{4,12},{8,16},{12,20},{16,24},{20,28},{24,32},{28,36},{32,40... | collective-permute-start | bytes 884744 | tf_op jit(solution)/shard_map/ppermute | solution.py:241
  21.9 4.0 %collective-permute-start.10 = (bf16[4,16,2304]{2,1,0:T(8,128)(2,1)S(1)}, bf16[4,16,2304]{2,1,0:T(8,128)(2,1)S(1)}, u32[]{:S(2)}, u32[]{:S(2)}) collective-permute-start(bf16[4,16,2304]{2,1,0:T(8,128)(2,1)S(1)} %pad_maximum_fusion.12), channel_id=1, source_target_pairs={{0,56},{4,60},{8,0},{12,4},{16,8},{20,12},{24,16},{28,20},{32,24},... | collective-permute-start | bytes 884744 | tf_op jit(solution)/shard_map/ppermute | solution.py:241
  25.9 0.1 collective-permute-start.6
  26.0 8.5 %collective-permute-done.9.refs_5_ = bf16[4,16,2304]{2,1,0:T(8,128)(2,1)S(1)} collective-permute-done((bf16[4,16,2304]{2,1,0:T(8,128)(2,1)S(1)}, bf16[4,16,2304]{2,1,0:T(8,128)(2,1)S(1)}, u32[]{:S(2)}, u32[]{:S(2)}) %collective-permute-start.9) | collective-permute-done | bytes 294944 | tf_op jit(solution)/shard_map/ppermute | solution.py:241
  34.5 0.0 collective-permute-done.10.refs_6_
  34.5 0.1 pad_maximum_fusion.5
  34.6 0.1 collective-permute-start.15
  34.7 3.2 %collective-permute-start.11 = (bf16[8,16,2304]{2,1,0:T(8,128)(2,1)S(1)}, bf16[8,16,2304]{2,1,0:T(8,128)(2,1)S(1)}, u32[]{:S(2)}, u32[]{:S(2)}) collective-permute-start(bf16[8,16,2304]{2,1,0:T(8,128)(2,1)S(1)} %get-tuple-element.33), channel_id=1, source_target_pairs={{0,64},{64,128},{128,192},{192,0},{1,65},{65,129},{129,193},{193,1... | collective-permute-start | bytes 1769480 | tf_op jit(solution)/shard_map/ppermute | solution.py:241
  38.0 0.0 collective-permute-done.14.refs_1_
  38.0 8.1 %collective-permute-start.7 = (bf16[4,16,2304]{2,1,0:T(8,128)(2,1)S(1)}, bf16[4,16,2304]{2,1,0:T(8,128)(2,1)S(1)}, u32[]{:S(2)}, u32[]{:S(2)}) collective-permute-start(bf16[4,16,2304]{2,1,0:T(8,128)(2,1)S(1)} %pad_maximum_fusion.9), channel_id=1, source_target_pairs={{0,48},{4,52},{8,56},{12,60},{16,0},{20,4},{24,8},{28,12},{32,16},... | collective-permute-start | bytes 884744 | tf_op jit(solution)/shard_map/ppermute | solution.py:241
  46.1 2.0 %collective-permute-done.15.refs_4_ = bf16[8,16,2304]{2,1,0:T(8,128)(2,1)S(1)} collective-permute-done((bf16[8,16,2304]{2,1,0:T(8,128)(2,1)S(1)}, bf16[8,16,2304]{2,1,0:T(8,128)(2,1)S(1)}, u32[]{:S(2)}, u32[]{:S(2)}) %collective-permute-start.15) | collective-permute-done | bytes 589856 | tf_op jit(solution)/shard_map/ppermute | solution.py:241
  48.2 0.0 collective-permute-done.11.refs_3_
  48.3 2.9 %collective-permute-done.7.refs_10_ = bf16[4,16,2304]{2,1,0:T(8,128)(2,1)S(1)} collective-permute-done((bf16[4,16,2304]{2,1,0:T(8,128)(2,1)S(1)}, bf16[4,16,2304]{2,1,0:T(8,128)(2,1)S(1)}, u32[]{:S(2)}, u32[]{:S(2)}) %collective-permute-start.7) | collective-permute-done | bytes 294944 | tf_op jit(solution)/shard_map/ppermute | solution.py:241
  51.2 0.3 pad_maximum_fusion.1
  51.5 0.4 copy-done.12
  51.9 0.0 collective-permute-start.16
  51.9 3.2 %collective-permute-start.12 = (bf16[14,16,2304]{2,1,0:T(8,128)(2,1)S(1)}, bf16[14,16,2304]{2,1,0:T(8,128)(2,1)S(1)}, u32[]{:S(2)}, u32[]{:S(2)}) collective-permute-start(bf16[14,16,2304]{2,1,0:T(8,128)(2,1)S(1)} %get-tuple-element.31), channel_id=1, source_target_pairs={{0,64},{64,128},{128,192},{192,0},{1,65},{65,129},{129,193},{193,1... | collective-permute-start | bytes 3096584 | tf_op jit(solution)/shard_map/ppermute | solution.py:241
  55.2 5.5 %collective-permute-start.4 = (bf16[4,16,2304]{2,1,0:T(8,128)(2,1)S(1)}, bf16[4,16,2304]{2,1,0:T(8,128)(2,1)S(1)}, u32[]{:S(2)}, u32[]{:S(2)}) collective-permute-start(bf16[4,16,2304]{2,1,0:T(8,128)(2,1)S(1)} %pad_maximum_fusion.6), channel_id=1, source_target_pairs={{0,24},{4,28},{8,32},{12,36},{16,40},{20,44},{24,48},{28,52},{32,5... | collective-permute-start | bytes 884744 | tf_op jit(solution)/shard_map/ppermute | solution.py:241
  60.7 0.1 collective-permute-start.5
  60.8 10.6 %collective-permute-done.16.refs_8_ = bf16[14,16,2304]{2,1,0:T(8,128)(2,1)S(1)} collective-permute-done((bf16[14,16,2304]{2,1,0:T(8,128)(2,1)S(1)}, bf16[14,16,2304]{2,1,0:T(8,128)(2,1)S(1)}, u32[]{:S(2)}, u32[]{:S(2)}) %collective-permute-start.16) | collective-permute-done | bytes 1032224 | tf_op jit(solution)/shard_map/ppermute | solution.py:241
  71.5 0.0 copy-start.23
  71.5 4.5 %collective-permute-done.5.refs_3_ = bf16[4,16,2304]{2,1,0:T(8,128)(2,1)S(1)} collective-permute-done((bf16[4,16,2304]{2,1,0:T(8,128)(2,1)S(1)}, bf16[4,16,2304]{2,1,0:T(8,128)(2,1)S(1)}, u32[]{:S(2)}, u32[]{:S(2)}) %collective-permute-start.5) | collective-permute-done | bytes 294944 | tf_op jit(solution)/shard_map/ppermute | solution.py:241
  76.0 1.1 pad_maximum_fusion.3
  77.1 0.1 collective-permute-start.17
  77.2 3.2 %collective-permute-start.13 = (bf16[12,16,2304]{2,1,0:T(8,128)(2,1)S(1)}, bf16[12,16,2304]{2,1,0:T(8,128)(2,1)S(1)}, u32[]{:S(2)}, u32[]{:S(2)}) collective-permute-start(bf16[12,16,2304]{2,1,0:T(8,128)(2,1)S(1)} %get-tuple-element.29), channel_id=1, source_target_pairs={{0,64},{64,128},{128,192},{192,0},{1,65},{65,129},{129,193},{193,1... | collective-permute-start | bytes 2654216 | tf_op jit(solution)/shard_map/ppermute | solution.py:241
  80.4 0.1 stack.67
  80.5 0.6 convert_reduce_fusion
  81.2 2.5 %collective-permute-start.18 = (bf16[4,16,2304]{2,1,0:T(8,128)(2,1)S(1)}, bf16[4,16,2304]{2,1,0:T(8,128)(2,1)S(1)}, u32[]{:S(2)}, u32[]{:S(2)}) collective-permute-start(bf16[4,16,2304]{2,1,0:T(8,128)(2,1)S(1)} %pad_maximum_fusion.13), channel_id=1, source_target_pairs={{0,32},{4,36},{8,40},{12,44},{16,48},{20,52},{24,56},{28,60},{32,0... | collective-permute-start | bytes 884744 | tf_op jit(solution)/shard_map/ppermute | solution.py:241
  83.7 0.1 select_reduce_fusion.1
  83.8 0.1 iota_compare_fusion.1
  83.9 10.8 %collective-permute-done.18.refs_8_ = bf16[4,16,2304]{2,1,0:T(8,128)(2,1)S(1)} collective-permute-done((bf16[4,16,2304]{2,1,0:T(8,128)(2,1)S(1)}, bf16[4,16,2304]{2,1,0:T(8,128)(2,1)S(1)}, u32[]{:S(2)}, u32[]{:S(2)}) %collective-permute-start.18) | collective-permute-done | bytes 294944 | tf_op jit(solution)/shard_map/ppermute | solution.py:241
  94.7 0.0 collective-permute-start.23
  94.7 3.2 %collective-permute-start.19 = (bf16[4,16,2304]{2,1,0:T(8,128)(2,1)S(1)}, bf16[4,16,2304]{2,1,0:T(8,128)(2,1)}, u32[]{:S(2)}, u32[]{:S(2)}) collective-permute-start(bf16[4,16,2304]{2,1,0:T(8,128)(2,1)S(1)} %collective-permute-done.18.refs_8_), channel_id=1, source_target_pairs={{0,64},{64,128},{128,192},{192,0},{1,65},{65,129},{129,193},{193,1... | collective-permute-start | bytes 884744 | tf_op jit(solution)/shard_map/ppermute | solution.py:241
  97.9 0.3 collective-permute-done.17.refs_1_
  98.2 0.1 collective-permute-start.22
  98.3 3.3 %collective-permute-done.13.refs_0_ = bf16[12,16,2304]{2,1,0:T(8,128)(2,1)S(1)} collective-permute-done((bf16[12,16,2304]{2,1,0:T(8,128)(2,1)S(1)}, bf16[12,16,2304]{2,1,0:T(8,128)(2,1)S(1)}, u32[]{:S(2)}, u32[]{:S(2)}) %collective-permute-start.13) | collective-permute-done | bytes 884768 | tf_op jit(solution)/shard_map/ppermute | solution.py:241
  101.7 3.9 %collective-permute-start.20 = (bf16[4,16,2304]{2,1,0:T(8,128)(2,1)S(1)}, bf16[4,16,2304]{2,1,0:T(8,128)(2,1)S(1)}, u32[]{:S(2)}, u32[]{:S(2)}) collective-permute-start(bf16[4,16,2304]{2,1,0:T(8,128)(2,1)S(1)} %slice.106), channel_id=1, source_target_pairs={{0,64},{64,128},{128,192},{192,0},{1,65},{65,129},{129,193},{193,1... | collective-permute-start | bytes 884744 | tf_op jit(solution)/shard_map/ppermute | solution.py:241
  105.6 0.1 select_reduce_fusion
  105.7 0.1 copy.8
  105.8 0.7 reshape.68.dest_ref
  106.5 6.7 %shard_map.66.refs_10_ = bf16[32,4,1,16,2304]{4,3,2,1,0:T(8,128)(2,1)} custom-call(s32[32]{0:T(128)} %reshape.68.dest_ref, s32[1]{0:T(128)} %bitcast.16.count_ref, s32[1]{0:T(128)} %bitcast.17.relay_ref, bf16[4,16,2304]{2,1,0:T(8,128)(2,1)} %copy-done.19, bf16[4,16,2304]{2,1,0:T(8,128)(2,1)} %copy-done.18, bf16[4,16,2304]{2,1,0:T(8,128)(2,1)} %copy-done.17, ...), custom_call_target="tpu_custom_call" | custom-call | bytes 10616832 | tf_op jit(solution)/shard_map/pallas_call | solution.py:226
  113.3 0.7 copy-done.21
  114.0 0.7 copy-done.22
  114.7 4.9 %shard_map.67 = bf16[32,4,1,16,2304]{4,3,2,1,0:T(8,128)(2,1)} custom-call(s32[32]{0:T(128)} %reshape.68.dest_ref, s32[1]{0:T(128)} %bitcast.16.count_ref, s32[1]{0:T(128)} %bitcast.17.relay_ref, bf16[12,16,2304]{2,1,0:T(8,128)(2,1)} %copy-done.8, bf16[12,16,2304]{2,1,0:T(8,128)(2,1)} %copy-done.7, ...), custom_call_target="tpu_custom_call", output_to_operand_aliasing={{}: (13, {})} | custom-call | bytes 8257536 | tf_op jit(solution)/shard_map/pallas_call | solution.py:226
  (68 shorter events, 0.5 us)
Async XLA Ops:
  0.0 10.0 %collective-permute-start.2 = (bf16[3,64,192]{2,1,0:T(8,128)(2,1)}, bf16[3,64,192]{2,1,0:T(8,128)(2,1)S(1)}, u32[]{:S(2)}, u32[]{:S(2)}) collective-permute-start(bf16[3,64,192]{2,1,0:T(8,128)(2,1)} %bitcast.34), channel_id=1, source_target_pairs={{0,3},{1,0},{2,1},{3,2},{4,7},{5,4},{6,5},{7,6},{8,11},{9,8},{10,9... | collective-permute-start | bytes 221192 | tf_op jit(solution)/shard_map/ppermute | solution.py:241
  3.0 7.1 %collective-permute-start.1 = (bf16[3,64,192]{2,1,0:T(8,128)(2,1)}, bf16[3,64,192]{2,1,0:T(8,128)(2,1)S(1)}, u32[]{:S(2)}, u32[]{:S(2)}) collective-permute-start(bf16[3,64,192]{2,1,0:T(8,128)(2,1)} %bitcast.35), channel_id=1, source_target_pairs={{0,2},{1,3},{2,0},{3,1},{4,6},{5,7},{6,4},{7,5},{8,10},{9,11},{10,... | collective-permute-start | bytes 221192 | tf_op jit(solution)/shard_map/ppermute | solution.py:241
  3.6 7.4 %collective-permute-start = (bf16[3,64,192]{2,1,0:T(8,128)(2,1)}, bf16[3,64,192]{2,1,0:T(8,128)(2,1)S(1)}, u32[]{:S(2)}, u32[]{:S(2)}) collective-permute-start(bf16[3,64,192]{2,1,0:T(8,128)(2,1)} %bitcast.36), channel_id=1, source_target_pairs={{0,1},{1,2},{2,3},{3,0},{4,5},{5,6},{6,7},{7,4},{8,9},{9,10},{10,1... | collective-permute-start | bytes 221192 | tf_op jit(solution)/shard_map/ppermute | solution.py:241
  6.2 1.0 copy-start
  7.2 1.0 copy-start.1
  8.2 1.0 copy-start.2
  9.2 1.9 %copy-start.3 = (bf16[1,3,256,64]{2,3,1,0:T(8,128)(2,1)S(1)}, bf16[1,3,256,64]{2,3,1,0:T(8,128)(2,1)}, u32[]{:S(2)}) copy-start(bf16[1,3,256,64]{2,3,1,0:T(8,128)(2,1)} %param.9) | copy-start | bytes 294916
  9.2 1.9 %copy-start.4 = (bf16[1,3,64,192]{3,2,1,0:T(8,128)(2,1)S(1)}, bf16[1,3,64,192]{3,2,1,0:T(8,128)(2,1)}, u32[]{:S(2)}) copy-start(bf16[1,3,64,192]{3,2,1,0:T(8,128)(2,1)} %param.10) | copy-start | bytes 221188
  13.4 2.9 %collective-permute-start.3 = (bf16[16,16,2304]{2,1,0:T(8,128)(2,1)S(1)}, bf16[16,16,2304]{2,1,0:T(8,128)(2,1)S(1)}, u32[]{:S(2)}, u32[]{:S(2)}) collective-permute-start(bf16[16,16,2304]{2,1,0:T(8,128)(2,1)S(1)} %get-tuple-element.9), channel_id=1, source_target_pairs={{0,4},{4,0},{8,12},{12,8},{16,20},{20,16},{24,28},{28,24},{32,36},... | collective-permute-start | bytes 3538952 | tf_op jit(solution)/shard_map/ppermute | solution.py:272
  16.5 18.1 %copy-start.17 = (bf16[4,16,2304]{2,1,0:T(8,128)(2,1)}, bf16[4,16,2304]{2,1,0:T(8,128)(2,1)S(1)}, u32[]{:S(2)}) copy-start(bf16[4,16,2304]{2,1,0:T(8,128)(2,1)S(1)} %pad_maximum_fusion.10.refs_2_) | copy-start | bytes 884740
  16.5 21.5 %collective-permute-start.14 = (bf16[4,16,2304]{2,1,0:T(8,128)(2,1)S(1)}, bf16[4,16,2304]{2,1,0:T(8,128)(2,1)S(1)}, u32[]{:S(2)}, u32[]{:S(2)}) collective-permute-start(bf16[4,16,2304]{2,1,0:T(8,128)(2,1)S(1)} %pad_maximum_fusion.10.refs_2_), channel_id=1, source_target_pairs={{0,192},{64,0},{128,64},{192,128},{1,193},{65,1},{129,65},{193,129... | collective-permute-start | bytes 884744 | tf_op jit(solution)/shard_map/ppermute | solution.py:241
  17.4 28.7 %collective-permute-start.8 = (bf16[4,16,2304]{2,1,0:T(8,128)(2,1)S(1)}, bf16[4,16,2304]{2,1,0:T(8,128)(2,1)S(1)}, u32[]{:S(2)}, u32[]{:S(2)}) collective-permute-start(bf16[4,16,2304]{2,1,0:T(8,128)(2,1)S(1)} %pad_maximum_fusion.10.refs_2_), channel_id=1, source_target_pairs={{0,64},{64,128},{128,192},{192,0},{1,65},{65,129},{129,193},{193,1... | collective-permute-start | bytes 884744 | tf_op jit(solution)/shard_map/ppermute | solution.py:241
  19.8 14.6 %collective-permute-start.9 = (bf16[4,16,2304]{2,1,0:T(8,128)(2,1)S(1)}, bf16[4,16,2304]{2,1,0:T(8,128)(2,1)S(1)}, u32[]{:S(2)}, u32[]{:S(2)}) collective-permute-start(bf16[4,16,2304]{2,1,0:T(8,128)(2,1)S(1)} %pad_maximum_fusion.11), channel_id=1, source_target_pairs={{0,8},{4,12},{8,16},{12,20},{16,24},{20,28},{24,32},{28,36},{32,40... | collective-permute-start | bytes 884744 | tf_op jit(solution)/shard_map/ppermute | solution.py:241
  21.9 12.6 %collective-permute-start.10 = (bf16[4,16,2304]{2,1,0:T(8,128)(2,1)S(1)}, bf16[4,16,2304]{2,1,0:T(8,128)(2,1)S(1)}, u32[]{:S(2)}, u32[]{:S(2)}) collective-permute-start(bf16[4,16,2304]{2,1,0:T(8,128)(2,1)S(1)} %pad_maximum_fusion.12), channel_id=1, source_target_pairs={{0,56},{4,60},{8,0},{12,4},{16,8},{20,12},{24,16},{28,20},{32,24},... | collective-permute-start | bytes 884744 | tf_op jit(solution)/shard_map/ppermute | solution.py:241
  25.9 22.3 %collective-permute-start.6 = (bf16[4,16,2304]{2,1,0:T(8,128)(2,1)S(1)}, bf16[4,16,2304]{2,1,0:T(8,128)(2,1)S(1)}, u32[]{:S(2)}, u32[]{:S(2)}) collective-permute-start(bf16[4,16,2304]{2,1,0:T(8,128)(2,1)S(1)} %pad_maximum_fusion.8), channel_id=1, source_target_pairs={{0,16},{4,20},{8,24},{12,28},{16,32},{20,36},{24,40},{28,44},{32,4... | collective-permute-start | bytes 884744 | tf_op jit(solution)/shard_map/ppermute | solution.py:241
  34.5 3.5 %copy-start.15 = (bf16[4,16,2304]{2,1,0:T(8,128)(2,1)}, bf16[4,16,2304]{2,1,0:T(8,128)(2,1)S(1)}, u32[]{:S(2)}) copy-start(bf16[4,16,2304]{2,1,0:T(8,128)(2,1)S(1)} %collective-permute-done.9.refs_5_) | copy-start | bytes 884740
  34.5 3.5 %copy-start.16 = (bf16[4,16,2304]{2,1,0:T(8,128)(2,1)}, bf16[4,16,2304]{2,1,0:T(8,128)(2,1)S(1)}, u32[]{:S(2)}) copy-start(bf16[4,16,2304]{2,1,0:T(8,128)(2,1)S(1)} %collective-permute-done.10.refs_6_) | copy-start | bytes 884740
  34.6 13.5 %collective-permute-start.15 = (bf16[8,16,2304]{2,1,0:T(8,128)(2,1)S(1)}, bf16[8,16,2304]{2,1,0:T(8,128)(2,1)S(1)}, u32[]{:S(2)}, u32[]{:S(2)}) collective-permute-start(bf16[8,16,2304]{2,1,0:T(8,128)(2,1)S(1)} %get-tuple-element.32), channel_id=1, source_target_pairs={{0,192},{64,0},{128,64},{192,128},{1,193},{65,1},{129,65},{193,129... | collective-permute-start | bytes 1769480 | tf_op jit(solution)/shard_map/ppermute | solution.py:241
  34.7 13.5 %collective-permute-start.11 = (bf16[8,16,2304]{2,1,0:T(8,128)(2,1)S(1)}, bf16[8,16,2304]{2,1,0:T(8,128)(2,1)S(1)}, u32[]{:S(2)}, u32[]{:S(2)}) collective-permute-start(bf16[8,16,2304]{2,1,0:T(8,128)(2,1)S(1)} %get-tuple-element.33), channel_id=1, source_target_pairs={{0,64},{64,128},{128,192},{192,0},{1,65},{65,129},{129,193},{193,1... | collective-permute-start | bytes 1769480 | tf_op jit(solution)/shard_map/ppermute | solution.py:241
  38.0 10.3 %copy-start.18 = (bf16[4,16,2304]{2,1,0:T(8,128)(2,1)}, bf16[4,16,2304]{2,1,0:T(8,128)(2,1)S(1)}, u32[]{:S(2)}) copy-start(bf16[4,16,2304]{2,1,0:T(8,128)(2,1)S(1)} %collective-permute-done.14.refs_1_) | copy-start | bytes 884740
  38.0 13.2 %collective-permute-start.7 = (bf16[4,16,2304]{2,1,0:T(8,128)(2,1)S(1)}, bf16[4,16,2304]{2,1,0:T(8,128)(2,1)S(1)}, u32[]{:S(2)}, u32[]{:S(2)}) collective-permute-start(bf16[4,16,2304]{2,1,0:T(8,128)(2,1)S(1)} %pad_maximum_fusion.9), channel_id=1, source_target_pairs={{0,48},{4,52},{8,56},{12,60},{16,0},{20,4},{24,8},{28,12},{32,16},... | collective-permute-start | bytes 884744 | tf_op jit(solution)/shard_map/ppermute | solution.py:241
  46.1 2.2 %copy-start.19 = (bf16[4,16,2304]{2,1,0:T(8,128)(2,1)}, bf16[4,16,2304]{2,1,0:T(8,128)(2,1)S(1)}, u32[]{:S(2)}) copy-start(bf16[4,16,2304]{2,1,0:T(8,128)(2,1)S(1)} %collective-permute-done.8.refs_0_) | copy-start | bytes 884740
  48.1 3.3 %copy-start.9 = (bf16[8,16,2304]{2,1,0:T(8,128)(2,1)}, bf16[8,16,2304]{2,1,0:T(8,128)(2,1)S(1)}, u32[]{:S(2)}) copy-start(bf16[8,16,2304]{2,1,0:T(8,128)(2,1)S(1)} %collective-permute-done.15.refs_4_) | copy-start | bytes 1769476
  48.2 3.3 %copy-start.10 = (bf16[8,16,2304]{2,1,0:T(8,128)(2,1)}, bf16[8,16,2304]{2,1,0:T(8,128)(2,1)S(1)}, u32[]{:S(2)}) copy-start(bf16[8,16,2304]{2,1,0:T(8,128)(2,1)S(1)} %collective-permute-done.11.refs_3_) | copy-start | bytes 1769476
  48.2 3.2 %copy-start.11 = (bf16[4,16,2304]{2,1,0:T(8,128)(2,1)}, bf16[4,16,2304]{2,1,0:T(8,128)(2,1)S(1)}, u32[]{:S(2)}) copy-start(bf16[4,16,2304]{2,1,0:T(8,128)(2,1)S(1)} %collective-permute-done.6.refs_9_) | copy-start | bytes 884740
  51.2 0.7 copy-start.12
  51.9 19.5 %collective-permute-start.16 = (bf16[14,16,2304]{2,1,0:T(8,128)(2,1)S(1)}, bf16[14,16,2304]{2,1,0:T(8,128)(2,1)S(1)}, u32[]{:S(2)}, u32[]{:S(2)}) collective-permute-start(bf16[14,16,2304]{2,1,0:T(8,128)(2,1)S(1)} %get-tuple-element.30), channel_id=1, source_target_pairs={{0,192},{64,0},{128,64},{192,128},{1,193},{65,1},{129,65},{193,129... | collective-permute-start | bytes 3096584 | tf_op jit(solution)/shard_map/ppermute | solution.py:241
  51.9 19.5 %collective-permute-start.12 = (bf16[14,16,2304]{2,1,0:T(8,128)(2,1)S(1)}, bf16[14,16,2304]{2,1,0:T(8,128)(2,1)S(1)}, u32[]{:S(2)}, u32[]{:S(2)}) collective-permute-start(bf16[14,16,2304]{2,1,0:T(8,128)(2,1)S(1)} %get-tuple-element.31), channel_id=1, source_target_pairs={{0,64},{64,128},{128,192},{192,0},{1,65},{65,129},{129,193},{193,1... | collective-permute-start | bytes 3096584 | tf_op jit(solution)/shard_map/ppermute | solution.py:241
  55.2 16.3 %collective-permute-start.4 = (bf16[4,16,2304]{2,1,0:T(8,128)(2,1)S(1)}, bf16[4,16,2304]{2,1,0:T(8,128)(2,1)S(1)}, u32[]{:S(2)}, u32[]{:S(2)}) collective-permute-start(bf16[4,16,2304]{2,1,0:T(8,128)(2,1)S(1)} %pad_maximum_fusion.6), channel_id=1, source_target_pairs={{0,24},{4,28},{8,32},{12,36},{16,40},{20,44},{24,48},{28,52},{32,5... | collective-permute-start | bytes 884744 | tf_op jit(solution)/shard_map/ppermute | solution.py:241
  60.7 15.3 %collective-permute-start.5 = (bf16[4,16,2304]{2,1,0:T(8,128)(2,1)S(1)}, bf16[4,16,2304]{2,1,0:T(8,128)(2,1)S(1)}, u32[]{:S(2)}, u32[]{:S(2)}) collective-permute-start(bf16[4,16,2304]{2,1,0:T(8,128)(2,1)S(1)} %pad_maximum_fusion.7), channel_id=1, source_target_pairs={{0,40},{4,44},{8,48},{12,52},{16,56},{20,60},{24,0},{28,4},{32,8},... | collective-permute-start | bytes 884744 | tf_op jit(solution)/shard_map/ppermute | solution.py:241
  71.4 5.7 %copy-start.5 = (bf16[14,16,2304]{2,1,0:T(8,128)(2,1)}, bf16[14,16,2304]{2,1,0:T(8,128)(2,1)S(1)}, u32[]{:S(2)}) copy-start(bf16[14,16,2304]{2,1,0:T(8,128)(2,1)S(1)} %collective-permute-done.16.refs_8_) | copy-start | bytes 3096580
  71.4 5.7 %copy-start.6 = (bf16[14,16,2304]{2,1,0:T(8,128)(2,1)}, bf16[14,16,2304]{2,1,0:T(8,128)(2,1)S(1)}, u32[]{:S(2)}) copy-start(bf16[14,16,2304]{2,1,0:T(8,128)(2,1)S(1)} %collective-permute-done.12.refs_7_) | copy-start | bytes 3096580
  71.5 9.1 %copy-start.23 = (s32[16,16]{1,0:T(8,128)S(1)}, s32[16,16]{1,0:T(8,128)}, u32[]{:S(2)}) copy-start(s32[16,16]{1,0:T(8,128)} %param.11) | copy-start | bytes 3076
  71.5 5.6 %copy-start.13 = (bf16[4,16,2304]{2,1,0:T(8,128)(2,1)}, bf16[4,16,2304]{2,1,0:T(8,128)(2,1)S(1)}, u32[]{:S(2)}) copy-start(bf16[4,16,2304]{2,1,0:T(8,128)(2,1)S(1)} %collective-permute-done.4.refs_2_) | copy-start | bytes 884740
  76.0 1.1 copy-start.14
  77.1 21.1 %collective-permute-start.17 = (bf16[12,16,2304]{2,1,0:T(8,128)(2,1)}, bf16[12,16,2304]{2,1,0:T(8,128)(2,1)S(1)}, u32[]{:S(2)}, u32[]{:S(2)}) collective-permute-start(bf16[12,16,2304]{2,1,0:T(8,128)(2,1)} %get-tuple-element.28), channel_id=1, source_target_pairs={{0,192},{64,0},{128,64},{192,128},{1,193},{65,1},{129,65},{193,129... | collective-permute-start | bytes 2654216 | tf_op jit(solution)/shard_map/ppermute | solution.py:241
  77.2 24.4 %collective-permute-start.13 = (bf16[12,16,2304]{2,1,0:T(8,128)(2,1)S(1)}, bf16[12,16,2304]{2,1,0:T(8,128)(2,1)S(1)}, u32[]{:S(2)}, u32[]{:S(2)}) collective-permute-start(bf16[12,16,2304]{2,1,0:T(8,128)(2,1)S(1)} %get-tuple-element.29), channel_id=1, source_target_pairs={{0,64},{64,128},{128,192},{192,0},{1,65},{65,129},{129,193},{193,1... | collective-permute-start | bytes 2654216 | tf_op jit(solution)/shard_map/ppermute | solution.py:241
  81.2 13.5 %collective-permute-start.18 = (bf16[4,16,2304]{2,1,0:T(8,128)(2,1)S(1)}, bf16[4,16,2304]{2,1,0:T(8,128)(2,1)S(1)}, u32[]{:S(2)}, u32[]{:S(2)}) collective-permute-start(bf16[4,16,2304]{2,1,0:T(8,128)(2,1)S(1)} %pad_maximum_fusion.13), channel_id=1, source_target_pairs={{0,32},{4,36},{8,40},{12,44},{16,48},{20,52},{24,56},{28,60},{32,0... | collective-permute-start | bytes 884744 | tf_op jit(solution)/shard_map/ppermute | solution.py:241
  94.7 18.5 %copy-start.20 = (bf16[4,16,2304]{2,1,0:T(8,128)(2,1)}, bf16[4,16,2304]{2,1,0:T(8,128)(2,1)S(1)}, u32[]{:S(2)}) copy-start(bf16[4,16,2304]{2,1,0:T(8,128)(2,1)S(1)} %collective-permute-done.18.refs_8_) | copy-start | bytes 884740
  94.7 18.6 %collective-permute-start.23 = (bf16[4,16,2304]{2,1,0:T(8,128)(2,1)S(1)}, bf16[4,16,2304]{2,1,0:T(8,128)(2,1)S(1)}, u32[]{:S(2)}, u32[]{:S(2)}) collective-permute-start(bf16[4,16,2304]{2,1,0:T(8,128)(2,1)S(1)} %collective-permute-done.18.refs_8_), channel_id=1, source_target_pairs={{0,128},{64,192},{128,0},{192,64},{1,129},{65,193},{129,1},{193,65... | collective-permute-start | bytes 884744 | tf_op jit(solution)/shard_map/ppermute | solution.py:241
  94.7 18.6 %collective-permute-start.21 = (bf16[4,16,2304]{2,1,0:T(8,128)(2,1)S(1)}, bf16[4,16,2304]{2,1,0:T(8,128)(2,1)}, u32[]{:S(2)}, u32[]{:S(2)}) collective-permute-start(bf16[4,16,2304]{2,1,0:T(8,128)(2,1)S(1)} %collective-permute-done.18.refs_8_), channel_id=1, source_target_pairs={{0,192},{64,0},{128,64},{192,128},{1,193},{65,1},{129,65},{193,129... | collective-permute-start | bytes 884744 | tf_op jit(solution)/shard_map/ppermute | solution.py:241
  94.7 18.6 %collective-permute-start.19 = (bf16[4,16,2304]{2,1,0:T(8,128)(2,1)S(1)}, bf16[4,16,2304]{2,1,0:T(8,128)(2,1)}, u32[]{:S(2)}, u32[]{:S(2)}) collective-permute-start(bf16[4,16,2304]{2,1,0:T(8,128)(2,1)S(1)} %collective-permute-done.18.refs_8_), channel_id=1, source_target_pairs={{0,64},{64,128},{128,192},{192,0},{1,65},{65,129},{129,193},{193,1... | collective-permute-start | bytes 884744 | tf_op jit(solution)/shard_map/ppermute | solution.py:241
  98.2 15.0 %copy-start.7 = (bf16[12,16,2304]{2,1,0:T(8,128)(2,1)}, bf16[12,16,2304]{2,1,0:T(8,128)(2,1)S(1)}, u32[]{:S(2)}) copy-start(bf16[12,16,2304]{2,1,0:T(8,128)(2,1)S(1)} %collective-permute-done.17.refs_1_) | copy-start | bytes 2654212
  98.2 15.0 %collective-permute-start.22 = (bf16[4,16,2304]{2,1,0:T(8,128)(2,1)S(1)}, bf16[4,16,2304]{2,1,0:T(8,128)(2,1)}, u32[]{:S(2)}, u32[]{:S(2)}) collective-permute-start(bf16[4,16,2304]{2,1,0:T(8,128)(2,1)S(1)} %slice.107), channel_id=1, source_target_pairs={{0,192},{64,0},{128,64},{192,128},{1,193},{65,1},{129,65},{193,129... | collective-permute-start | bytes 884744 | tf_op jit(solution)/shard_map/ppermute | solution.py:241
  101.6 11.6 %copy-start.8 = (bf16[12,16,2304]{2,1,0:T(8,128)(2,1)}, bf16[12,16,2304]{2,1,0:T(8,128)(2,1)S(1)}, u32[]{:S(2)}) copy-start(bf16[12,16,2304]{2,1,0:T(8,128)(2,1)S(1)} %collective-permute-done.13.refs_0_) | copy-start | bytes 2654212
  101.7 11.6 %collective-permute-start.20 = (bf16[4,16,2304]{2,1,0:T(8,128)(2,1)S(1)}, bf16[4,16,2304]{2,1,0:T(8,128)(2,1)S(1)}, u32[]{:S(2)}, u32[]{:S(2)}) collective-permute-start(bf16[4,16,2304]{2,1,0:T(8,128)(2,1)S(1)} %slice.106), channel_id=1, source_target_pairs={{0,64},{64,128},{128,192},{192,0},{1,65},{65,129},{129,193},{193,1... | collective-permute-start | bytes 884744 | tf_op jit(solution)/shard_map/ppermute | solution.py:241
  113.3 0.7 copy-start.21
  114.0 0.7 copy-start.22

commit v3 on v2

--- a/solution.py
+++ b/solution.py
@@ -285,7 +285,7 @@
         ([1, chips - 1], None, False, False, 1),
         ([2, chips - 2], None, False, True, 1),
         ([3, chips - 3], None, False, False, 1),
-        ([4], None, True, True, 0),
+        ([4], None, False, True, 0),
     ]
     sources = jnp.stack(
         [((me - 2 * d) % owners) ^ core for names, *_ in steps for d in names for core in (0, 1)]

time: 121 us -> 120 us (level)
  starting transfers between devices: 47.4 us -> 45.5 us
  local copies, waits for them, and re-layouts: 6.74 us -> 8.54 us
    unnamed x48 -> x50, local copies, waits for them, and re-layouts: 4.9 us -> 6.77 us
    ppermute x23 -> x21, starting transfers between devices: 47.3 us -> 45.4 us  [shift(): lax.ppermute(value, axis, [(i, (i + by) % size) for i in range(size)])]
    ppermute x23 -> x21, waiting for transfers between devices: 44 us -> 42.8 us  [shift(): lax.ppermute(value, axis, [(i, (i + by) % size) for i in range(size)])]
  transfers between devices with their start and end apart: 24 -> 22, of which waited for: 10 -> 9; matrix products, arithmetic and copies ran while one was open for 3% -> 3% of each run, Pallas kernels for 6% -> 7%
where the time goes in v3:
time: 120 us; the launch traced here: 119 us
  starting transfers between devices  45.5 us (38%)
  waiting for transfers between devices  45.5 us (38%)
  Pallas kernels  15.7 us (13%)
  local copies, waits for them, and re-layouts  8.54 us (7%)
  other arithmetic  2.7 us (2%)
    ppermute x21, starting transfers between devices, shift(): lax.ppermute(value, axis, [(i, (i + by) % size) for i in range(size)])  45.4 us
    ppermute x21, waiting for transfers between devices, shift(): lax.ppermute(value, axis, [(i, (i + by) % size) for i in range(size)])  42.8 us
    pallas_call x2, Pallas kernels, place(): pl.pallas_call(functools.partial(place_kernel, pieces, count, first), out...  12.6 us
    unnamed x50, local copies, waits for them, and re-layouts  6.77 us
    ppermute x1, waiting for transfers between devices, body(): got = lax.ppermute(swap, 'expert', mate)  2.75 us
  transfers between devices with their start and end apart: 22, of which 9 were waited for; matrix products, arithmetic and copies ran while one was open for 3% of the time, Pallas kernels for 7%

profile of v3, /device:TPU:6, one launch (start us, length us, event | category | flops | bytes accessed | tf_op | source)
XLA Modules:
  0.0 118.7 jit_solution(1703044347919897366)
XLA Ops:
  0.0 3.0 %collective-permute-start.2 = (bf16[3,64,192]{2,1,0:T(8,128)(2,1)}, bf16[3,64,192]{2,1,0:T(8,128)(2,1)S(1)}, u32[]{:S(2)}, u32[]{:S(2)}) collective-permute-start(bf16[3,64,192]{2,1,0:T(8,128)(2,1)} %bitcast.34), channel_id=1, source_target_pairs={{0,3},{1,0},{2,1},{3,2},{4,7},{5,4},{6,5},{7,6},{8,11},{9,8},{10,9... | collective-permute-start | bytes 221192 | tf_op jit(solution)/shard_map/ppermute | solution.py:241
  3.0 0.6 collective-permute-start.1
  3.6 1.0 collective-permute-start
  4.6 0.7 dynamic-slice_bitcast_fusion
  5.3 0.2 convert_reduce_fusion.2
  5.5 0.7 fusion.3.index_ref
  6.2 1.0 copy-done
  7.2 1.0 copy-done.1
  8.2 1.0 copy-done.2
  9.2 0.8 shard_map.64.woven_ref
  10.0 0.0 collective-permute-done.2.v3
  10.0 0.0 collective-permute-done.1.v2
  10.1 1.0 collective-permute-done.v1
  11.1 2.3 %shard_map.65 = (bf16[2,16,2304]{2,1,0:T(8,128)(2,1)S(1)}, bf16[14,16,2304]{2,1,0:T(8,128)(2,1)S(1)}, bf16[16,16,2304]{2,1,0:T(8,128)(2,1)S(1)}) custom-call(s32[16]{0:T(128)S(1)} %fusion.3.index_ref, s32[1]{0:T(128)} %bitcast.19.tensor_ref, bf16[256,2304]{1,0:T(8,128)(2,1)S(1)} %shard_map.64.woven_ref, bf16[3,64,256]{2,1,0:T(8,128)(2,1)S(1)} %bitcast.33, ...), custom_call_target="tpu_custom_call" | custom-call | flops 150994944 | bytes 4000000 | tf_op jit(solution)/shard_map/pallas_call | solution.py:140
  13.4 0.1 collective-permute-start.3
  13.5 0.1 fusion.6
  13.6 2.8 %collective-permute-done.3 = bf16[16,16,2304]{2,1,0:T(8,128)(2,1)S(1)} collective-permute-done((bf16[16,16,2304]{2,1,0:T(8,128)(2,1)S(1)}, bf16[16,16,2304]{2,1,0:T(8,128)(2,1)S(1)}, u32[]{:S(2)}, u32[]{:S(2)}) %collective-permute-start.3) | collective-permute-done | bytes 1179680 | tf_op jit(solution)/shard_map/ppermute | solution.py:272
  16.4 0.1 fusion.5
  16.5 0.9 collective-permute-start.14
  17.4 2.4 %collective-permute-start.8 = (bf16[4,16,2304]{2,1,0:T(8,128)(2,1)S(1)}, bf16[4,16,2304]{2,1,0:T(8,128)(2,1)S(1)}, u32[]{:S(2)}, u32[]{:S(2)}) collective-permute-start(bf16[4,16,2304]{2,1,0:T(8,128)(2,1)S(1)} %pad_maximum_fusion.12.refs_2_), channel_id=1, source_target_pairs={{0,64},{64,128},{128,192},{192,0},{1,65},{65,129},{129,193},{193,1... | collective-permute-start | bytes 884744 | tf_op jit(solution)/shard_map/ppermute | solution.py:241
  19.8 2.0 %collective-permute-start.9 = (bf16[4,16,2304]{2,1,0:T(8,128)(2,1)S(1)}, bf16[4,16,2304]{2,1,0:T(8,128)(2,1)S(1)}, u32[]{:S(2)}, u32[]{:S(2)}) collective-permute-start(bf16[4,16,2304]{2,1,0:T(8,128)(2,1)S(1)} %pad_maximum_fusion.13), channel_id=1, source_target_pairs={{0,8},{4,12},{8,16},{12,20},{16,24},{20,28},{24,32},{28,36},{32,40... | collective-permute-start | bytes 884744 | tf_op jit(solution)/shard_map/ppermute | solution.py:241
  21.9 4.0 %collective-permute-start.10 = (bf16[4,16,2304]{2,1,0:T(8,128)(2,1)S(1)}, bf16[4,16,2304]{2,1,0:T(8,128)(2,1)S(1)}, u32[]{:S(2)}, u32[]{:S(2)}) collective-permute-start(bf16[4,16,2304]{2,1,0:T(8,128)(2,1)S(1)} %pad_maximum_fusion.14), channel_id=1, source_target_pairs={{0,56},{4,60},{8,0},{12,4},{16,8},{20,12},{24,16},{28,20},{32,24},... | collective-permute-start | bytes 884744 | tf_op jit(solution)/shard_map/ppermute | solution.py:241
  25.9 0.1 collective-permute-start.6
  26.0 8.5 %collective-permute-done.9.refs_5_ = bf16[4,16,2304]{2,1,0:T(8,128)(2,1)S(1)} collective-permute-done((bf16[4,16,2304]{2,1,0:T(8,128)(2,1)S(1)}, bf16[4,16,2304]{2,1,0:T(8,128)(2,1)S(1)}, u32[]{:S(2)}, u32[]{:S(2)}) %collective-permute-start.9) | collective-permute-done | bytes 294944 | tf_op jit(solution)/shard_map/ppermute | solution.py:241
  34.5 0.0 collective-permute-done.10.refs_6_
  34.5 0.1 pad_maximum_fusion.7
  34.6 0.1 collective-permute-start.15
  34.7 3.2 %collective-permute-start.11 = (bf16[8,16,2304]{2,1,0:T(8,128)(2,1)S(1)}, bf16[8,16,2304]{2,1,0:T(8,128)(2,1)S(1)}, u32[]{:S(2)}, u32[]{:S(2)}) collective-permute-start(bf16[8,16,2304]{2,1,0:T(8,128)(2,1)S(1)} %get-tuple-element.33), channel_id=1, source_target_pairs={{0,64},{64,128},{128,192},{192,0},{1,65},{65,129},{129,193},{193,1... | collective-permute-start | bytes 1769480 | tf_op jit(solution)/shard_map/ppermute | solution.py:241
  38.0 0.0 collective-permute-done.14.refs_1_
  38.0 8.1 %collective-permute-start.7 = (bf16[4,16,2304]{2,1,0:T(8,128)(2,1)S(1)}, bf16[4,16,2304]{2,1,0:T(8,128)(2,1)S(1)}, u32[]{:S(2)}, u32[]{:S(2)}) collective-permute-start(bf16[4,16,2304]{2,1,0:T(8,128)(2,1)S(1)} %pad_maximum_fusion.11), channel_id=1, source_target_pairs={{0,48},{4,52},{8,56},{12,60},{16,0},{20,4},{24,8},{28,12},{32,16},... | collective-permute-start | bytes 884744 | tf_op jit(solution)/shard_map/ppermute | solution.py:241
  46.1 2.0 %collective-permute-done.15.refs_4_ = bf16[8,16,2304]{2,1,0:T(8,128)(2,1)S(1)} collective-permute-done((bf16[8,16,2304]{2,1,0:T(8,128)(2,1)S(1)}, bf16[8,16,2304]{2,1,0:T(8,128)(2,1)S(1)}, u32[]{:S(2)}, u32[]{:S(2)}) %collective-permute-start.15) | collective-permute-done | bytes 589856 | tf_op jit(solution)/shard_map/ppermute | solution.py:241
  48.3 2.9 %collective-permute-done.7.refs_10_ = bf16[4,16,2304]{2,1,0:T(8,128)(2,1)S(1)} collective-permute-done((bf16[4,16,2304]{2,1,0:T(8,128)(2,1)S(1)}, bf16[4,16,2304]{2,1,0:T(8,128)(2,1)S(1)}, u32[]{:S(2)}, u32[]{:S(2)}) %collective-permute-start.7) | collective-permute-done | bytes 294944 | tf_op jit(solution)/shard_map/ppermute | solution.py:241
  51.2 0.3 pad_maximum_fusion.1
  51.5 0.4 copy-done.12
  51.9 0.0 collective-permute-start.16
  51.9 3.2 %collective-permute-start.12 = (bf16[14,16,2304]{2,1,0:T(8,128)(2,1)S(1)}, bf16[14,16,2304]{2,1,0:T(8,128)(2,1)S(1)}, u32[]{:S(2)}, u32[]{:S(2)}) collective-permute-start(bf16[14,16,2304]{2,1,0:T(8,128)(2,1)S(1)} %get-tuple-element.31), channel_id=1, source_target_pairs={{0,64},{64,128},{128,192},{192,0},{1,65},{65,129},{129,193},{193,1... | collective-permute-start | bytes 3096584 | tf_op jit(solution)/shard_map/ppermute | solution.py:241
  55.2 5.5 %collective-permute-start.4 = (bf16[4,16,2304]{2,1,0:T(8,128)(2,1)S(1)}, bf16[4,16,2304]{2,1,0:T(8,128)(2,1)S(1)}, u32[]{:S(2)}, u32[]{:S(2)}) collective-permute-start(bf16[4,16,2304]{2,1,0:T(8,128)(2,1)S(1)} %pad_maximum_fusion.8), channel_id=1, source_target_pairs={{0,24},{4,28},{8,32},{12,36},{16,40},{20,44},{24,48},{28,52},{32,5... | collective-permute-start | bytes 884744 | tf_op jit(solution)/shard_map/ppermute | solution.py:241
  60.7 0.1 collective-permute-start.5
  60.8 11.0 %collective-permute-done.16.refs_8_ = bf16[14,16,2304]{2,1,0:T(8,128)(2,1)S(1)} collective-permute-done((bf16[14,16,2304]{2,1,0:T(8,128)(2,1)S(1)}, bf16[14,16,2304]{2,1,0:T(8,128)(2,1)S(1)}, u32[]{:S(2)}, u32[]{:S(2)}) %collective-permute-start.16) | collective-permute-done | bytes 1032224 | tf_op jit(solution)/shard_map/ppermute | solution.py:241
  71.9 0.0 copy-start.24
  71.9 4.1 %collective-permute-done.5.refs_3_ = bf16[4,16,2304]{2,1,0:T(8,128)(2,1)S(1)} collective-permute-done((bf16[4,16,2304]{2,1,0:T(8,128)(2,1)S(1)}, bf16[4,16,2304]{2,1,0:T(8,128)(2,1)S(1)}, u32[]{:S(2)}, u32[]{:S(2)}) %collective-permute-start.5) | collective-permute-done | bytes 294944 | tf_op jit(solution)/shard_map/ppermute | solution.py:241
  76.1 0.2 pad_maximum_fusion.3
  76.3 0.5 copy-done.14
  76.8 3.2 %collective-permute-start.13 = (bf16[12,16,2304]{2,1,0:T(8,128)(2,1)S(1)}, bf16[12,16,2304]{2,1,0:T(8,128)(2,1)S(1)}, u32[]{:S(2)}, u32[]{:S(2)}) collective-permute-start(bf16[12,16,2304]{2,1,0:T(8,128)(2,1)S(1)} %get-tuple-element.29), channel_id=1, source_target_pairs={{0,64},{64,128},{128,192},{192,0},{1,65},{65,129},{129,193},{193,1... | collective-permute-start | bytes 2654216 | tf_op jit(solution)/shard_map/ppermute | solution.py:241
  80.0 3.2 %collective-permute-start.18 = (bf16[4,16,2304]{2,1,0:T(8,128)(2,1)S(1)}, bf16[4,16,2304]{2,1,0:T(8,128)(2,1)S(1)}, u32[]{:S(2)}, u32[]{:S(2)}) collective-permute-start(bf16[4,16,2304]{2,1,0:T(8,128)(2,1)S(1)} %pad_maximum_fusion.15), channel_id=1, source_target_pairs={{0,32},{4,36},{8,40},{12,44},{16,48},{20,52},{24,56},{28,60},{32,0... | collective-permute-start | bytes 884744 | tf_op jit(solution)/shard_map/ppermute | solution.py:241
  83.2 0.6 convert_reduce_fusion
  83.9 11.3 %collective-permute-done.17.refs_1_ = bf16[12,16,2304]{2,1,0:T(8,128)(2,1)S(1)} collective-permute-done((bf16[12,16,2304]{2,1,0:T(8,128)(2,1)S(1)}, bf16[12,16,2304]{2,1,0:T(8,128)(2,1)S(1)}, u32[]{:S(2)}, u32[]{:S(2)}) %collective-permute-start.17) | collective-permute-done | bytes 884768 | tf_op jit(solution)/shard_map/ppermute | solution.py:241
  95.2 0.1 pad_maximum_fusion.4
  95.3 0.7 copy-done.7
  96.0 0.3 copy-done.8
  96.3 3.2 %collective-permute-start.19 = (bf16[8,16,2304]{2,1,0:T(8,128)(2,1)S(1)}, bf16[8,16,2304]{2,1,0:T(8,128)(2,1)S(1)}, u32[]{:S(2)}, u32[]{:S(2)}) collective-permute-start(bf16[8,16,2304]{2,1,0:T(8,128)(2,1)S(1)} %get-tuple-element.35), channel_id=1, source_target_pairs={{0,64},{64,128},{128,192},{192,0},{1,65},{65,129},{129,193},{193,1... | collective-permute-start | bytes 1769480 | tf_op jit(solution)/shard_map/ppermute | solution.py:241
  99.6 0.1 select_reduce_fusion.1
  99.8 0.1 stack.67
  99.9 0.1 iota_compare_fusion.1
  100.0 1.5 %collective-permute-start.21 = (bf16[4,16,2304]{2,1,0:T(8,128)(2,1)S(1)}, bf16[4,16,2304]{2,1,0:T(8,128)(2,1)S(1)}, u32[]{:S(2)}, u32[]{:S(2)}) collective-permute-start(bf16[4,16,2304]{2,1,0:T(8,128)(2,1)S(1)} %collective-permute-done.18.refs_6_), channel_id=1, source_target_pairs={{0,128},{64,192},{128,0},{192,64},{1,129},{65,193},{129,1},{193,65... | collective-permute-start | bytes 884744 | tf_op jit(solution)/shard_map/ppermute | solution.py:241
  101.5 0.1 select_reduce_fusion
  101.6 0.1 copy.8
  101.7 0.6 reshape.68.dest_ref
  102.3 7.9 %shard_map.66.refs_8_ = bf16[32,4,1,16,2304]{4,3,2,1,0:T(8,128)(2,1)} custom-call(s32[32]{0:T(128)} %reshape.68.dest_ref, s32[1]{0:T(128)} %bitcast.16.count_ref, s32[1]{0:T(128)} %bitcast.17.relay_ref, bf16[4,16,2304]{2,1,0:T(8,128)(2,1)} %copy-done.20, bf16[4,16,2304]{2,1,0:T(8,128)(2,1)} %copy-done.19, bf16[4,16,2304]{2,1,0:T(8,128)(2,1)} %copy-done.17, ...), custom_call_target="tpu_custom_call" | custom-call | bytes 10616832 | tf_op jit(solution)/shard_map/pallas_call | solution.py:226
  110.2 1.9 %collective-permute-done.21.refs_7_ = bf16[4,16,2304]{2,1,0:T(8,128)(2,1)S(1)} collective-permute-done((bf16[4,16,2304]{2,1,0:T(8,128)(2,1)S(1)}, bf16[4,16,2304]{2,1,0:T(8,128)(2,1)S(1)}, u32[]{:S(2)}, u32[]{:S(2)}) %collective-permute-start.21) | collective-permute-done | bytes 294944 | tf_op jit(solution)/shard_map/ppermute | solution.py:241
  112.1 0.7 copy-done.23
  112.8 0.3 copy-done.21
  113.0 0.8 copy-done.22
  113.8 4.7 %shard_map.67 = bf16[32,4,1,16,2304]{4,3,2,1,0:T(8,128)(2,1)} custom-call(s32[32]{0:T(128)} %reshape.68.dest_ref, s32[1]{0:T(128)} %bitcast.16.count_ref, s32[1]{0:T(128)} %bitcast.17.relay_ref, bf16[12,16,2304]{2,1,0:T(8,128)(2,1)} %copy-done.8, bf16[12,16,2304]{2,1,0:T(8,128)(2,1)} %copy-done.7, ...), custom_call_target="tpu_custom_call", output_to_operand_aliasing={{}: (11, {})} | custom-call | bytes 8257536 | tf_op jit(solution)/shard_map/pallas_call | solution.py:226
  (67 shorter events, 0.5 us)
Async XLA Ops:
  0.0 10.0 %collective-permute-start.2 = (bf16[3,64,192]{2,1,0:T(8,128)(2,1)}, bf16[3,64,192]{2,1,0:T(8,128)(2,1)S(1)}, u32[]{:S(2)}, u32[]{:S(2)}) collective-permute-start(bf16[3,64,192]{2,1,0:T(8,128)(2,1)} %bitcast.34), channel_id=1, source_target_pairs={{0,3},{1,0},{2,1},{3,2},{4,7},{5,4},{6,5},{7,6},{8,11},{9,8},{10,9... | collective-permute-start | bytes 221192 | tf_op jit(solution)/shard_map/ppermute | solution.py:241
  3.0 7.1 %collective-permute-start.1 = (bf16[3,64,192]{2,1,0:T(8,128)(2,1)}, bf16[3,64,192]{2,1,0:T(8,128)(2,1)S(1)}, u32[]{:S(2)}, u32[]{:S(2)}) collective-permute-start(bf16[3,64,192]{2,1,0:T(8,128)(2,1)} %bitcast.35), channel_id=1, source_target_pairs={{0,2},{1,3},{2,0},{3,1},{4,6},{5,7},{6,4},{7,5},{8,10},{9,11},{10,... | collective-permute-start | bytes 221192 | tf_op jit(solution)/shard_map/ppermute | solution.py:241
  3.6 7.4 %collective-permute-start = (bf16[3,64,192]{2,1,0:T(8,128)(2,1)}, bf16[3,64,192]{2,1,0:T(8,128)(2,1)S(1)}, u32[]{:S(2)}, u32[]{:S(2)}) collective-permute-start(bf16[3,64,192]{2,1,0:T(8,128)(2,1)} %bitcast.36), channel_id=1, source_target_pairs={{0,1},{1,2},{2,3},{3,0},{4,5},{5,6},{6,7},{7,4},{8,9},{9,10},{10,1... | collective-permute-start | bytes 221192 | tf_op jit(solution)/shard_map/ppermute | solution.py:241
  6.2 1.0 copy-start
  7.2 1.0 copy-start.1
  8.2 1.0 copy-start.2
  9.2 1.9 %copy-start.3 = (bf16[1,3,256,64]{2,3,1,0:T(8,128)(2,1)S(1)}, bf16[1,3,256,64]{2,3,1,0:T(8,128)(2,1)}, u32[]{:S(2)}) copy-start(bf16[1,3,256,64]{2,3,1,0:T(8,128)(2,1)} %param.9) | copy-start | bytes 294916
  9.2 1.9 %copy-start.4 = (bf16[1,3,64,192]{3,2,1,0:T(8,128)(2,1)S(1)}, bf16[1,3,64,192]{3,2,1,0:T(8,128)(2,1)}, u32[]{:S(2)}) copy-start(bf16[1,3,64,192]{3,2,1,0:T(8,128)(2,1)} %param.10) | copy-start | bytes 221188
  13.4 2.9 %collective-permute-start.3 = (bf16[16,16,2304]{2,1,0:T(8,128)(2,1)S(1)}, bf16[16,16,2304]{2,1,0:T(8,128)(2,1)S(1)}, u32[]{:S(2)}, u32[]{:S(2)}) collective-permute-start(bf16[16,16,2304]{2,1,0:T(8,128)(2,1)S(1)} %get-tuple-element.9), channel_id=1, source_target_pairs={{0,4},{4,0},{8,12},{12,8},{16,20},{20,16},{24,28},{28,24},{32,36},... | collective-permute-start | bytes 3538952 | tf_op jit(solution)/shard_map/ppermute | solution.py:272
  16.5 18.1 %copy-start.17 = (bf16[4,16,2304]{2,1,0:T(8,128)(2,1)}, bf16[4,16,2304]{2,1,0:T(8,128)(2,1)S(1)}, u32[]{:S(2)}) copy-start(bf16[4,16,2304]{2,1,0:T(8,128)(2,1)S(1)} %pad_maximum_fusion.12.refs_2_) | copy-start | bytes 884740
  16.5 21.5 %collective-permute-start.14 = (bf16[4,16,2304]{2,1,0:T(8,128)(2,1)S(1)}, bf16[4,16,2304]{2,1,0:T(8,128)(2,1)S(1)}, u32[]{:S(2)}, u32[]{:S(2)}) collective-permute-start(bf16[4,16,2304]{2,1,0:T(8,128)(2,1)S(1)} %pad_maximum_fusion.12.refs_2_), channel_id=1, source_target_pairs={{0,192},{64,0},{128,64},{192,128},{1,193},{65,1},{129,65},{193,129... | collective-permute-start | bytes 884744 | tf_op jit(solution)/shard_map/ppermute | solution.py:241
  17.4 28.7 %collective-permute-start.8 = (bf16[4,16,2304]{2,1,0:T(8,128)(2,1)S(1)}, bf16[4,16,2304]{2,1,0:T(8,128)(2,1)S(1)}, u32[]{:S(2)}, u32[]{:S(2)}) collective-permute-start(bf16[4,16,2304]{2,1,0:T(8,128)(2,1)S(1)} %pad_maximum_fusion.12.refs_2_), channel_id=1, source_target_pairs={{0,64},{64,128},{128,192},{192,0},{1,65},{65,129},{129,193},{193,1... | collective-permute-start | bytes 884744 | tf_op jit(solution)/shard_map/ppermute | solution.py:241
  19.8 14.6 %collective-permute-start.9 = (bf16[4,16,2304]{2,1,0:T(8,128)(2,1)S(1)}, bf16[4,16,2304]{2,1,0:T(8,128)(2,1)S(1)}, u32[]{:S(2)}, u32[]{:S(2)}) collective-permute-start(bf16[4,16,2304]{2,1,0:T(8,128)(2,1)S(1)} %pad_maximum_fusion.13), channel_id=1, source_target_pairs={{0,8},{4,12},{8,16},{12,20},{16,24},{20,28},{24,32},{28,36},{32,40... | collective-permute-start | bytes 884744 | tf_op jit(solution)/shard_map/ppermute | solution.py:241
  21.9 12.6 %collective-permute-start.10 = (bf16[4,16,2304]{2,1,0:T(8,128)(2,1)S(1)}, bf16[4,16,2304]{2,1,0:T(8,128)(2,1)S(1)}, u32[]{:S(2)}, u32[]{:S(2)}) collective-permute-start(bf16[4,16,2304]{2,1,0:T(8,128)(2,1)S(1)} %pad_maximum_fusion.14), channel_id=1, source_target_pairs={{0,56},{4,60},{8,0},{12,4},{16,8},{20,12},{24,16},{28,20},{32,24},... | collective-permute-start | bytes 884744 | tf_op jit(solution)/shard_map/ppermute | solution.py:241
  25.9 22.3 %collective-permute-start.6 = (bf16[4,16,2304]{2,1,0:T(8,128)(2,1)S(1)}, bf16[4,16,2304]{2,1,0:T(8,128)(2,1)S(1)}, u32[]{:S(2)}, u32[]{:S(2)}) collective-permute-start(bf16[4,16,2304]{2,1,0:T(8,128)(2,1)S(1)} %pad_maximum_fusion.10), channel_id=1, source_target_pairs={{0,16},{4,20},{8,24},{12,28},{16,32},{20,36},{24,40},{28,44},{32,4... | collective-permute-start | bytes 884744 | tf_op jit(solution)/shard_map/ppermute | solution.py:241
  34.5 3.5 %copy-start.15 = (bf16[4,16,2304]{2,1,0:T(8,128)(2,1)}, bf16[4,16,2304]{2,1,0:T(8,128)(2,1)S(1)}, u32[]{:S(2)}) copy-start(bf16[4,16,2304]{2,1,0:T(8,128)(2,1)S(1)} %collective-permute-done.9.refs_5_) | copy-start | bytes 884740
  34.5 3.5 %copy-start.16 = (bf16[4,16,2304]{2,1,0:T(8,128)(2,1)}, bf16[4,16,2304]{2,1,0:T(8,128)(2,1)S(1)}, u32[]{:S(2)}) copy-start(bf16[4,16,2304]{2,1,0:T(8,128)(2,1)S(1)} %collective-permute-done.10.refs_6_) | copy-start | bytes 884740
  34.6 13.5 %collective-permute-start.15 = (bf16[8,16,2304]{2,1,0:T(8,128)(2,1)S(1)}, bf16[8,16,2304]{2,1,0:T(8,128)(2,1)S(1)}, u32[]{:S(2)}, u32[]{:S(2)}) collective-permute-start(bf16[8,16,2304]{2,1,0:T(8,128)(2,1)S(1)} %get-tuple-element.32), channel_id=1, source_target_pairs={{0,192},{64,0},{128,64},{192,128},{1,193},{65,1},{129,65},{193,129... | collective-permute-start | bytes 1769480 | tf_op jit(solution)/shard_map/ppermute | solution.py:241
  34.7 13.5 %collective-permute-start.11 = (bf16[8,16,2304]{2,1,0:T(8,128)(2,1)S(1)}, bf16[8,16,2304]{2,1,0:T(8,128)(2,1)S(1)}, u32[]{:S(2)}, u32[]{:S(2)}) collective-permute-start(bf16[8,16,2304]{2,1,0:T(8,128)(2,1)S(1)} %get-tuple-element.33), channel_id=1, source_target_pairs={{0,64},{64,128},{128,192},{192,0},{1,65},{65,129},{129,193},{193,1... | collective-permute-start | bytes 1769480 | tf_op jit(solution)/shard_map/ppermute | solution.py:241
  38.0 10.3 %copy-start.19 = (bf16[4,16,2304]{2,1,0:T(8,128)(2,1)}, bf16[4,16,2304]{2,1,0:T(8,128)(2,1)S(1)}, u32[]{:S(2)}) copy-start(bf16[4,16,2304]{2,1,0:T(8,128)(2,1)S(1)} %collective-permute-done.14.refs_1_) | copy-start | bytes 884740
  38.0 13.2 %collective-permute-start.7 = (bf16[4,16,2304]{2,1,0:T(8,128)(2,1)S(1)}, bf16[4,16,2304]{2,1,0:T(8,128)(2,1)S(1)}, u32[]{:S(2)}, u32[]{:S(2)}) collective-permute-start(bf16[4,16,2304]{2,1,0:T(8,128)(2,1)S(1)} %pad_maximum_fusion.11), channel_id=1, source_target_pairs={{0,48},{4,52},{8,56},{12,60},{16,0},{20,4},{24,8},{28,12},{32,16},... | collective-permute-start | bytes 884744 | tf_op jit(solution)/shard_map/ppermute | solution.py:241
  46.1 2.2 %copy-start.20 = (bf16[4,16,2304]{2,1,0:T(8,128)(2,1)}, bf16[4,16,2304]{2,1,0:T(8,128)(2,1)S(1)}, u32[]{:S(2)}) copy-start(bf16[4,16,2304]{2,1,0:T(8,128)(2,1)S(1)} %collective-permute-done.8.refs_0_) | copy-start | bytes 884740
  48.1 3.3 %copy-start.9 = (bf16[8,16,2304]{2,1,0:T(8,128)(2,1)}, bf16[8,16,2304]{2,1,0:T(8,128)(2,1)S(1)}, u32[]{:S(2)}) copy-start(bf16[8,16,2304]{2,1,0:T(8,128)(2,1)S(1)} %collective-permute-done.15.refs_4_) | copy-start | bytes 1769476
  48.2 3.3 %copy-start.10 = (bf16[8,16,2304]{2,1,0:T(8,128)(2,1)}, bf16[8,16,2304]{2,1,0:T(8,128)(2,1)S(1)}, u32[]{:S(2)}) copy-start(bf16[8,16,2304]{2,1,0:T(8,128)(2,1)S(1)} %collective-permute-done.11.refs_3_) | copy-start | bytes 1769476
  48.3 3.2 %copy-start.11 = (bf16[4,16,2304]{2,1,0:T(8,128)(2,1)}, bf16[4,16,2304]{2,1,0:T(8,128)(2,1)S(1)}, u32[]{:S(2)}) copy-start(bf16[4,16,2304]{2,1,0:T(8,128)(2,1)S(1)} %collective-permute-done.6.refs_9_) | copy-start | bytes 884740
  51.2 0.7 copy-start.12
  51.9 19.9 %collective-permute-start.16 = (bf16[14,16,2304]{2,1,0:T(8,128)(2,1)S(1)}, bf16[14,16,2304]{2,1,0:T(8,128)(2,1)S(1)}, u32[]{:S(2)}, u32[]{:S(2)}) collective-permute-start(bf16[14,16,2304]{2,1,0:T(8,128)(2,1)S(1)} %get-tuple-element.30), channel_id=1, source_target_pairs={{0,192},{64,0},{128,64},{192,128},{1,193},{65,1},{129,65},{193,129... | collective-permute-start | bytes 3096584 | tf_op jit(solution)/shard_map/ppermute | solution.py:241
  51.9 19.9 %collective-permute-start.12 = (bf16[14,16,2304]{2,1,0:T(8,128)(2,1)S(1)}, bf16[14,16,2304]{2,1,0:T(8,128)(2,1)S(1)}, u32[]{:S(2)}, u32[]{:S(2)}) collective-permute-start(bf16[14,16,2304]{2,1,0:T(8,128)(2,1)S(1)} %get-tuple-element.31), channel_id=1, source_target_pairs={{0,64},{64,128},{128,192},{192,0},{1,65},{65,129},{129,193},{193,1... | collective-permute-start | bytes 3096584 | tf_op jit(solution)/shard_map/ppermute | solution.py:241
  55.2 16.7 %collective-permute-start.4 = (bf16[4,16,2304]{2,1,0:T(8,128)(2,1)S(1)}, bf16[4,16,2304]{2,1,0:T(8,128)(2,1)S(1)}, u32[]{:S(2)}, u32[]{:S(2)}) collective-permute-start(bf16[4,16,2304]{2,1,0:T(8,128)(2,1)S(1)} %pad_maximum_fusion.8), channel_id=1, source_target_pairs={{0,24},{4,28},{8,32},{12,36},{16,40},{20,44},{24,48},{28,52},{32,5... | collective-permute-start | bytes 884744 | tf_op jit(solution)/shard_map/ppermute | solution.py:241
  60.7 15.4 %collective-permute-start.5 = (bf16[4,16,2304]{2,1,0:T(8,128)(2,1)S(1)}, bf16[4,16,2304]{2,1,0:T(8,128)(2,1)S(1)}, u32[]{:S(2)}, u32[]{:S(2)}) collective-permute-start(bf16[4,16,2304]{2,1,0:T(8,128)(2,1)S(1)} %pad_maximum_fusion.9), channel_id=1, source_target_pairs={{0,40},{4,44},{8,48},{12,52},{16,56},{20,60},{24,0},{28,4},{32,8},... | collective-permute-start | bytes 884744 | tf_op jit(solution)/shard_map/ppermute | solution.py:241
  71.8 4.4 %copy-start.5 = (bf16[14,16,2304]{2,1,0:T(8,128)(2,1)}, bf16[14,16,2304]{2,1,0:T(8,128)(2,1)S(1)}, u32[]{:S(2)}) copy-start(bf16[14,16,2304]{2,1,0:T(8,128)(2,1)S(1)} %collective-permute-done.16.refs_8_) | copy-start | bytes 3096580
  71.9 4.4 %copy-start.6 = (bf16[14,16,2304]{2,1,0:T(8,128)(2,1)}, bf16[14,16,2304]{2,1,0:T(8,128)(2,1)S(1)}, u32[]{:S(2)}) copy-start(bf16[14,16,2304]{2,1,0:T(8,128)(2,1)S(1)} %collective-permute-done.12.refs_7_) | copy-start | bytes 3096580
  71.9 11.3 %copy-start.24 = (s32[16,16]{1,0:T(8,128)S(1)}, s32[16,16]{1,0:T(8,128)}, u32[]{:S(2)}) copy-start(s32[16,16]{1,0:T(8,128)} %param.11) | copy-start | bytes 3076
  71.9 4.4 %copy-start.13 = (bf16[4,16,2304]{2,1,0:T(8,128)(2,1)}, bf16[4,16,2304]{2,1,0:T(8,128)(2,1)S(1)}, u32[]{:S(2)}) copy-start(bf16[4,16,2304]{2,1,0:T(8,128)(2,1)S(1)} %collective-permute-done.4.refs_2_) | copy-start | bytes 884740
  76.0 0.7 copy-start.14
  76.8 18.3 %collective-permute-start.17 = (bf16[12,16,2304]{2,1,0:T(8,128)(2,1)S(1)}, bf16[12,16,2304]{2,1,0:T(8,128)(2,1)S(1)}, u32[]{:S(2)}, u32[]{:S(2)}) collective-permute-start(bf16[12,16,2304]{2,1,0:T(8,128)(2,1)S(1)} %get-tuple-element.28), channel_id=1, source_target_pairs={{0,192},{64,0},{128,64},{192,128},{1,193},{65,1},{129,65},{193,129... | collective-permute-start | bytes 2654216 | tf_op jit(solution)/shard_map/ppermute | solution.py:241
  76.8 18.4 %collective-permute-start.13 = (bf16[12,16,2304]{2,1,0:T(8,128)(2,1)S(1)}, bf16[12,16,2304]{2,1,0:T(8,128)(2,1)S(1)}, u32[]{:S(2)}, u32[]{:S(2)}) collective-permute-start(bf16[12,16,2304]{2,1,0:T(8,128)(2,1)S(1)} %get-tuple-element.29), channel_id=1, source_target_pairs={{0,64},{64,128},{128,192},{192,0},{1,65},{65,129},{129,193},{193,1... | collective-permute-start | bytes 2654216 | tf_op jit(solution)/shard_map/ppermute | solution.py:241
  80.0 15.2 %collective-permute-start.18 = (bf16[4,16,2304]{2,1,0:T(8,128)(2,1)S(1)}, bf16[4,16,2304]{2,1,0:T(8,128)(2,1)S(1)}, u32[]{:S(2)}, u32[]{:S(2)}) collective-permute-start(bf16[4,16,2304]{2,1,0:T(8,128)(2,1)S(1)} %pad_maximum_fusion.15), channel_id=1, source_target_pairs={{0,32},{4,36},{8,40},{12,44},{16,48},{20,52},{24,56},{28,60},{32,0... | collective-permute-start | bytes 884744 | tf_op jit(solution)/shard_map/ppermute | solution.py:241
  95.1 0.9 copy-start.7
  95.2 1.2 copy-start.8
  95.2 15.0 %copy-start.18 = (bf16[4,16,2304]{2,1,0:T(8,128)(2,1)}, bf16[4,16,2304]{2,1,0:T(8,128)(2,1)S(1)}, u32[]{:S(2)}) copy-start(bf16[4,16,2304]{2,1,0:T(8,128)(2,1)S(1)} %collective-permute-done.18.refs_6_) | copy-start | bytes 884740
  96.3 15.7 %collective-permute-start.20 = (bf16[8,16,2304]{2,1,0:T(8,128)(2,1)S(1)}, bf16[8,16,2304]{2,1,0:T(8,128)(2,1)S(1)}, u32[]{:S(2)}, u32[]{:S(2)}) collective-permute-start(bf16[8,16,2304]{2,1,0:T(8,128)(2,1)S(1)} %get-tuple-element.34), channel_id=1, source_target_pairs={{0,192},{64,0},{128,64},{192,128},{1,193},{65,1},{129,65},{193,129... | collective-permute-start | bytes 1769480 | tf_op jit(solution)/shard_map/ppermute | solution.py:241
  96.3 15.7 %collective-permute-start.19 = (bf16[8,16,2304]{2,1,0:T(8,128)(2,1)S(1)}, bf16[8,16,2304]{2,1,0:T(8,128)(2,1)S(1)}, u32[]{:S(2)}, u32[]{:S(2)}) collective-permute-start(bf16[8,16,2304]{2,1,0:T(8,128)(2,1)S(1)} %get-tuple-element.35), channel_id=1, source_target_pairs={{0,64},{64,128},{128,192},{192,0},{1,65},{65,129},{129,193},{193,1... | collective-permute-start | bytes 1769480 | tf_op jit(solution)/shard_map/ppermute | solution.py:241
  100.0 12.1 %collective-permute-start.21 = (bf16[4,16,2304]{2,1,0:T(8,128)(2,1)S(1)}, bf16[4,16,2304]{2,1,0:T(8,128)(2,1)S(1)}, u32[]{:S(2)}, u32[]{:S(2)}) collective-permute-start(bf16[4,16,2304]{2,1,0:T(8,128)(2,1)S(1)} %collective-permute-done.18.refs_6_), channel_id=1, source_target_pairs={{0,128},{64,192},{128,0},{192,64},{1,129},{65,193},{129,1},{193,65... | collective-permute-start | bytes 884744 | tf_op jit(solution)/shard_map/ppermute | solution.py:241
  112.0 0.7 copy-start.23
  112.1 1.0 copy-start.21
  113.0 0.8 copy-start.22
